TPU v7x, 128 devices: a whole 4x4x4 slice. The times are simulated.
128 devices in a mesh: dp: 8 (over x_hi, z), tensor: 16 (over x_lo, y, core).
Axes of the slice: x: 4 (x_hi: 2, x_lo: 2; x = x_hi * 2 + x_lo), y: 4, z: 4, core: 2. Of those that a mesh axis runs over, the one named last changes fastest.
Arguments:
- history: bfloat16 [17, 16384, 2048], P(None, ('dp', 'tensor')), may hold values from -6 to 6
- cotangent: bfloat16 [16384, 2048], P(('dp', 'tensor')), may hold values from -6 to 6
- lengths: int32 [8, 4], replicated, may hold values from 0 to 2048, as said below
- mix_gain: float32 [2048], replicated, may hold values from 0.5 to 1.5
- mix_first: float32 [2048, 68], replicated, may hold values from -0.125 to 0.125
- mix_second: float32 [68, 68], replicated, may hold values from -0.3 to 0.3
- mix_bias: float32 [68], replicated, may hold values from -1.8 to 1.8
- gain_query: float32 [2048], replicated, may hold values from 0.5 to 1.5
- gain_key: float32 [2048], replicated, may hold values from 0.5 to 1.5
- gain_value: float32 [2048], replicated, may hold values from 0.5 to 1.5
- gain_mlp: float32 [2048], replicated, may hold values from 0.5 to 1.5
- w_query: bfloat16 [2048, 2048], P(None, 'tensor'), may hold values from -0.125 to 0.125
- w_key: bfloat16 [2048, 2048], P(None, 'tensor'), may hold values from -0.125 to 0.125
- w_value: bfloat16 [2048, 2048], P(None, 'tensor'), may hold values from -0.125 to 0.125
- w_output: bfloat16 [2048, 2048], P('tensor'), may hold values from -1 to 1
- w_expand: bfloat16 [2048, 8192], P(None, 'tensor'), may hold values from -0.125 to 0.125
- w_reduce: bfloat16 [8192, 2048], P('tensor'), may hold values from -0.0625 to 0.0625
Outputs:
- output: bfloat16 [16384, 2048], P(('dp', 'tensor'))
- grad_history: bfloat16 [17, 16384, 2048], P(None, ('dp', 'tensor'))
- grad_mix_gain: float32 [2048], replicated
- grad_mix_first: float32 [2048, 68], replicated
- grad_mix_second: float32 [68, 68], replicated
- grad_mix_bias: float32 [68], replicated
- grad_gain_query: float32 [2048], replicated
- grad_gain_key: float32 [2048], replicated
- grad_gain_value: float32 [2048], replicated
- grad_gain_mlp: float32 [2048], replicated
- grad_w_query: float32 [2048, 2048], P('dp', 'tensor')
- grad_w_key: float32 [2048, 2048], P('dp', 'tensor')
- grad_w_value: float32 [2048, 2048], P('dp', 'tensor')
- grad_w_output: float32 [2048, 2048], P('tensor', 'dp')
- grad_w_expand: float32 [2048, 8192], P('dp', 'tensor')
- grad_w_reduce: float32 [8192, 2048], P('tensor', 'dp')
Inputs may be any that keep to these rules, and one draw needn't show every extreme that they name: Row g holds, in order, the lengths of the sequences packed into the 2048 tokens of data index g (0 marks an empty slot); each row sums to 2048, its longest entry is 1024 or more, and in some row one sequence fills all 2048 tokens.
All inputs are finite; a program needn't handle non-finite values.
Results may differ from a plain program's by a relative error of at most 0.019.
Values may be sent and summed in bfloat16 or wider, within the bound.
A program may use at most 320 MiB of HBM per device.

v0:
```python
import jax
import jax.numpy as jnp
from jax import lax
from jax.sharding import PartitionSpec as P

HEAD_DIM = 128
HISTORY = 17
STREAMS = 4
NORM_EPS = 1e-06
MASKED = -1e30
PRECISE = lax.Precision.HIGHEST


def swapped(x, axis, bit):
    return lax.ppermute(x, axis, [(i, i ^ 1 << bit) for i in range(lax.axis_size(axis))])


def rms_scale(values, gain_vector):
    inverse = lax.rsqrt(jnp.mean(values * values, axis=-1, keepdims=True) + NORM_EPS)
    return values * inverse * gain_vector


def matmul(left_side, right_side):
    return jnp.dot(left_side, right_side, precision=PRECISE)


def front_part(
    history_float, mix_gain, mix_first, mix_second, mix_bias, gain_query, gain_key, gain_value
):
    latest = rms_scale(history_float[HISTORY - 1], mix_gain)
    hidden = jax.nn.gelu(matmul(latest, mix_first), approximate=False)
    mixing = (matmul(hidden, mix_second) + mix_bias).reshape(
        history_float.shape[1], STREAMS, HISTORY
    )
    streams = jnp.einsum("tkj,jtd->ktd", mixing, history_float, precision=PRECISE)
    return (
        rms_scale(streams[0], gain_query),
        rms_scale(streams[1], gain_key),
        rms_scale(streams[2], gain_value),
        streams[3],
    )


def gelu_exact(values):
    return jax.nn.gelu(values, approximate=False)


def across_rows(left_side, right_side):
    return lax.dot_general(
        left_side, right_side, (((0,), (0,)), ((), ())), preferred_element_type=jnp.float32
    )


def across_cols(left_side, right_side):
    return lax.dot_general(
        left_side, right_side, (((1,), (1,)), ((), ())), preferred_element_type=jnp.float32
    )


def segment_of(places, doc_ends):
    return jnp.sum((places[:, None] >= doc_ends[None, :]).astype(jnp.int32), axis=1)


def gather_bits(piece, bit_list, join_dim, device_index):
    for bit_number in bit_list:
        partner = swapped(piece, "tensor", bit_number)
        upper = device_index // (1 << bit_number) % 2 == 1
        piece = jnp.where(
            upper,
            jnp.concatenate([partner, piece], axis=join_dim),
            jnp.concatenate([piece, partner], axis=join_dim),
        )
    return piece


def sum_bits(partial_value, bit_list, device_index, split_dim):
    for bit_number in reversed(bit_list):
        half_size = partial_value.shape[split_dim] // 2
        lower_half = lax.slice_in_dim(partial_value, 0, half_size, axis=split_dim)
        upper_half = lax.slice_in_dim(partial_value, half_size, 2 * half_size, axis=split_dim)
        upper = device_index // (1 << bit_number) % 2 == 1
        keep_half = jnp.where(upper, upper_half, lower_half)
        send_half = jnp.where(upper, lower_half, upper_half)
        partial_value = keep_half + swapped(
            send_half.astype(jnp.bfloat16), "tensor", bit_number
        ).astype(send_half.dtype)
    return partial_value


def make_scores(query_heads, key_heads, query_places, key_places, doc_ends):
    block_rows = min(512, query_heads.shape[0])
    scale_factor = HEAD_DIM ** (-0.5)
    query_segments = segment_of(query_places, doc_ends)
    key_segments = segment_of(key_places, doc_ends)

    def block_scores(block_index):
        scores = (
            jnp.einsum("qhd,khd->hqk", query_heads, key_heads, preferred_element_type=jnp.float32)
            * scale_factor
        )
        allowed = (query_places[:, None] >= key_places[None, :]) & (
            query_segments[:, None] == key_segments[None, :]
        )
        return (jnp.where(allowed[None], scores, MASKED), query_heads)

    return (block_scores, block_rows)


def on_device(
    history,
    cotangent,
    lengths,
    mix_gain,
    mix_first,
    mix_second,
    mix_bias,
    gain_query,
    gain_key,
    gain_value,
    gain_mlp,
    w_query,
    w_key,
    w_value,
    w_output,
    w_expand,
    w_reduce,
):
    shard_rows = history.shape[1]
    tensor_size = lax.axis_size("tensor")
    tok_group = shard_rows * tensor_size
    model_width = w_query.shape[0]
    tensor_index = lax.axis_index("tensor")
    low_bits = [0, 1]
    high_bits = list(range(2, tensor_size.bit_length() - 1))
    scale_factor = HEAD_DIM ** (-0.5)
    history_float = history.astype(jnp.float32)
    front_values, front_back = jax.vjp(
        front_part,
        history_float,
        mix_gain,
        mix_first,
        mix_second,
        mix_bias,
        gain_query,
        gain_key,
        gain_value,
    )
    query_norm, key_norm, value_norm, residual = front_values
    query_low = query_norm.astype(jnp.bfloat16)
    key_low = key_norm.astype(jnp.bfloat16)
    value_low = value_norm.astype(jnp.bfloat16)
    length_row = lax.dynamic_index_in_dim(lengths, lax.axis_index("dp"), 0, keepdims=False)
    doc_ends = jnp.cumsum(length_row)
    query_rows = gather_bits(query_low, high_bits, 0, tensor_index)
    key_rows = gather_bits(key_low, high_bits, 0, tensor_index)
    value_rows = gather_bits(value_low, high_bits, 0, tensor_index)
    cot_rows = gather_bits(cotangent, high_bits, 0, tensor_index)
    query_whole = gather_bits(w_query, low_bits, 1, tensor_index)
    key_whole = gather_bits(w_key, low_bits, 1, tensor_index)
    value_whole = gather_bits(w_value, low_bits, 1, tensor_index)
    output_whole = gather_bits(w_output, low_bits, 0, tensor_index)
    expand_whole = gather_bits(w_expand, low_bits, 1, tensor_index)
    reduce_whole = gather_bits(w_reduce, low_bits, 0, tensor_index)
    group_count = tensor_size // 4
    part_index = tensor_index % 4
    inner_rows = jnp.arange(shard_rows, dtype=jnp.int32)
    group_offsets = 4 * jnp.arange(group_count, dtype=jnp.int32)
    query_places = (
        (part_index + group_offsets)[:, None] * shard_rows + inner_rows[None, :]
    ).reshape(-1)
    key_places = (
        (jnp.arange(4, dtype=jnp.int32)[:, None, None] + group_offsets[None, :, None]) * shard_rows
        + inner_rows[None, None, :]
    ).reshape(-1)
    row_count = query_rows.shape[0]
    heads_here = query_whole.shape[1] // HEAD_DIM
    query_heads = (
        jnp.dot(query_rows, query_whole, preferred_element_type=jnp.float32)
        .astype(jnp.bfloat16)
        .reshape(row_count, heads_here, HEAD_DIM)
    )
    key_part = jnp.dot(key_rows, key_whole, preferred_element_type=jnp.float32).astype(jnp.bfloat16)
    value_part = jnp.dot(value_rows, value_whole, preferred_element_type=jnp.float32).astype(
        jnp.bfloat16
    )
    key_flat = gather_bits(key_part, low_bits, 0, tensor_index)
    value_flat = gather_bits(value_part, low_bits, 0, tensor_index)
    key_heads = key_flat.reshape(tok_group, heads_here, HEAD_DIM)
    value_heads = value_flat.reshape(tok_group, heads_here, HEAD_DIM)
    block_scores, block_rows = make_scores(
        query_heads, key_heads, query_places, key_places, doc_ends
    )
    block_count = row_count // block_rows

    def forward_block(block_index):
        masked, query_block = block_scores(block_index)
        top_score = jnp.max(masked, axis=-1, keepdims=True)
        exponent = jnp.exp(masked - top_score)
        row_total = jnp.sum(exponent, axis=-1, keepdims=True)
        weights_low = (exponent / row_total).astype(jnp.bfloat16)
        context_block = jnp.einsum(
            "hqk,khd->qhd", weights_low, value_heads, preferred_element_type=jnp.float32
        )
        return (context_block, top_score + jnp.log(row_total))

    context_blocks, log_totals = lax.map(forward_block, jnp.arange(block_count))
    context = context_blocks.reshape(row_count, heads_here * HEAD_DIM).astype(jnp.bfloat16)
    attended = sum_bits(
        jnp.dot(context, output_whole, preferred_element_type=jnp.float32),
        high_bits,
        tensor_index,
        0,
    )
    middle = residual + attended
    mlp_norm, norm_back = jax.vjp(rms_scale, middle, gain_mlp)
    mlp_low = mlp_norm.astype(jnp.bfloat16)
    mlp_gathered = gather_bits(mlp_low, high_bits, 0, tensor_index)
    expanded = jnp.dot(mlp_gathered, expand_whole, preferred_element_type=jnp.float32)
    activated, gelu_back = jax.vjp(gelu_exact, expanded)
    active_low = activated.astype(jnp.bfloat16)
    reduced = sum_bits(
        jnp.dot(active_low, reduce_whole, preferred_element_type=jnp.float32),
        high_bits,
        tensor_index,
        0,
    )
    output = (middle + reduced).astype(jnp.bfloat16)
    grad_w_reduce = across_rows(active_low, cot_rows)
    grad_active = across_cols(cot_rows, reduce_whole)
    (grad_expanded,) = gelu_back(grad_active)
    expand_low = grad_expanded.astype(jnp.bfloat16)
    grad_w_expand = across_rows(mlp_gathered, expand_low)
    grad_mlp_norm = sum_bits(across_cols(expand_low, expand_whole), high_bits, tensor_index, 0)
    grad_w_expand = sum_bits(grad_w_expand, low_bits, tensor_index, 1)
    grad_w_reduce = sum_bits(grad_w_reduce, low_bits, tensor_index, 0)
    grad_middle_norm, grad_gain_mlp = norm_back(grad_mlp_norm)
    grad_middle = cotangent.astype(jnp.float32) + grad_middle_norm
    middle_low = grad_middle.astype(jnp.bfloat16)
    middle_rows = gather_bits(middle_low, high_bits, 0, tensor_index)
    grad_w_output = across_rows(context, middle_rows)
    grad_context = (
        across_cols(middle_rows, output_whole)
        .astype(jnp.bfloat16)
        .reshape(row_count, heads_here, HEAD_DIM)
    )

    def backward_block(totals, block_index):
        grad_key_sum, grad_value_sum = totals
        masked, query_block = block_scores(block_index)
        weights_float = jnp.exp(masked - log_totals[block_index])
        weights_low = weights_float.astype(jnp.bfloat16)
        grad_weights = jnp.einsum(
            "qhd,khd->hqk", grad_context, value_heads, preferred_element_type=jnp.float32
        )
        row_delta = jnp.sum(grad_weights * weights_float, axis=-1, keepdims=True)
        grad_scores = (weights_float * (grad_weights - row_delta)).astype(jnp.bfloat16)
        grad_query_block = (
            jnp.einsum("hqk,khd->qhd", grad_scores, key_heads, preferred_element_type=jnp.float32)
            * scale_factor
        )
        grad_key_sum = (
            grad_key_sum
            + jnp.einsum(
                "hqk,qhd->khd", grad_scores, query_block, preferred_element_type=jnp.float32
            )
            * scale_factor
        )
        grad_value_sum = grad_value_sum + jnp.einsum(
            "hqk,qhd->khd", weights_low, grad_context, preferred_element_type=jnp.float32
        )
        return ((grad_key_sum, grad_value_sum), grad_query_block)

    zero_heads = jnp.zeros((tok_group, heads_here, HEAD_DIM), jnp.float32)
    (grad_key_sum, grad_value_sum), grad_query_blocks = lax.scan(
        backward_block, (zero_heads, zero_heads), jnp.arange(block_count)
    )
    grad_key_flat = grad_key_sum.reshape(tok_group, heads_here * HEAD_DIM)
    grad_value_flat = grad_value_sum.reshape(tok_group, heads_here * HEAD_DIM)
    grad_key_flat = sum_bits(grad_key_flat, low_bits, tensor_index, 0)
    grad_value_flat = sum_bits(grad_value_flat, low_bits, tensor_index, 0)
    grad_queries = grad_query_blocks.reshape(row_count, heads_here * HEAD_DIM).astype(jnp.bfloat16)
    grad_keys = grad_key_flat.astype(jnp.bfloat16)
    grad_values = grad_value_flat.astype(jnp.bfloat16)
    grad_w_query = across_rows(query_rows, grad_queries)
    grad_w_key = across_rows(key_rows, grad_keys)
    grad_w_value = across_rows(value_rows, grad_values)
    grad_w_query = sum_bits(grad_w_query, low_bits, tensor_index, 1)
    grad_w_key = sum_bits(grad_w_key, low_bits, tensor_index, 1)
    grad_w_value = sum_bits(grad_w_value, low_bits, tensor_index, 1)
    grad_w_output = sum_bits(grad_w_output, low_bits, tensor_index, 0)
    stream_partial = jnp.concatenate(
        [
            across_cols(grad_queries, query_whole),
            across_cols(grad_keys, key_whole),
            across_cols(grad_values, value_whole),
        ],
        axis=1,
    )
    grad_streams = sum_bits(stream_partial, high_bits, tensor_index, 0)
    front_grads = front_back(
        (
            grad_streams[:, :model_width],
            grad_streams[:, model_width : 2 * model_width],
            grad_streams[:, 2 * model_width :],
            grad_middle,
        )
    )
    grad_history = front_grads[0].astype(jnp.bfloat16)
    small_sums = lax.psum(
        (
            front_grads[1],
            front_grads[2],
            front_grads[3],
            front_grads[4],
            front_grads[5],
            front_grads[6],
            front_grads[7],
            grad_gain_mlp,
        ),
        ("dp", "tensor"),
    )
    sum_query, sum_key, sum_value, sum_output, sum_expand, sum_reduce = (
        lax.psum_scatter(
            grad_w_query.astype(jnp.bfloat16), "dp", scatter_dimension=0, tiled=True
        ).astype(jnp.float32),
        lax.psum_scatter(
            grad_w_key.astype(jnp.bfloat16), "dp", scatter_dimension=0, tiled=True
        ).astype(jnp.float32),
        lax.psum_scatter(
            grad_w_value.astype(jnp.bfloat16), "dp", scatter_dimension=0, tiled=True
        ).astype(jnp.float32),
        lax.psum_scatter(
            grad_w_output.astype(jnp.bfloat16), "dp", scatter_dimension=1, tiled=True
        ).astype(jnp.float32),
        lax.psum_scatter(
            grad_w_expand.astype(jnp.bfloat16), "dp", scatter_dimension=0, tiled=True
        ).astype(jnp.float32),
        lax.psum_scatter(
            grad_w_reduce.astype(jnp.bfloat16), "dp", scatter_dimension=1, tiled=True
        ).astype(jnp.float32),
    )
    return (
        output,
        grad_history,
        small_sums[0],
        small_sums[1],
        small_sums[2],
        small_sums[3],
        small_sums[4],
        small_sums[5],
        small_sums[6],
        small_sums[7],
        sum_query,
        sum_key,
        sum_value,
        sum_output,
        sum_expand,
        sum_reduce,
    )


def solution(mesh):
    placed = (
        P(None, ("dp", "tensor"), None),
        P(("dp", "tensor"), None),
        P(),
        P(),
        P(),
        P(),
        P(),
        P(),
        P(),
        P(),
        P(),
        P(None, "tensor"),
        P(None, "tensor"),
        P(None, "tensor"),
        P("tensor", None),
        P(None, "tensor"),
        P("tensor", None),
    )
    return jax.shard_map(
        on_device,
        mesh=mesh,
        in_specs=placed,
        out_specs=(
            P(("dp", "tensor"), None),
            P(None, ("dp", "tensor"), None),
            P(),
            P(),
            P(),
            P(),
            P(),
            P(),
            P(),
            P(),
            P("dp", "tensor"),
            P("dp", "tensor"),
            P("dp", "tensor"),
            P("tensor", "dp"),
            P("dp", "tensor"),
            P("tensor", "dp"),
        ),
        check_vma=False,
    )
```

profile of v0, /device:TPU:1, one launch (start us, length us, event | category | flops | bytes accessed | tf_op | source)
XLA Modules:
  0.0 1349.2 jit_solution(5649538605081657744)
XLA Ops:
  16.1 19.8 %fusion.22 = f32[4,128,2048]{2,0,1:T(4,128)S(1)} fusion(f32[128,4,17]{2,1,0:T(4,128)S(1)} %copy.62, bf16[17,128,2048]{2,1,0:T(8,128)(2,1)} %param.17), kind=kOutput, calls=%fused_computation.55 | convolution fusion | flops 213909504 | bytes 13142016 | tf_op jit(solution)/shard_map/jvp(tkj,jtd->ktd)/dot_general | solution.py:35
  51.3 16.1 %collective-permute-done.10 = bf16[128,2048]{1,0:T(8,128)(2,1)} collective-permute-done((bf16[128,2048]{1,0:T(8,128)(2,1)S(1)}, bf16[128,2048]{1,0:T(8,128)(2,1)}, u32[]{:S(2)}, u32[]{:S(2)}) %collective-permute-start.10) | collective-permute-done | bytes 524320 | tf_op jit(solution)/shard_map/ppermute | solution.py:15
  81.2 19.9 %collective-permute-done.6 = bf16[128,2048]{1,0:T(8,128)(2,1)S(1)} collective-permute-done((bf16[128,2048]{1,0:T(8,128)(2,1)S(1)}, bf16[128,2048]{1,0:T(8,128)(2,1)S(1)}, u32[]{:S(2)}, u32[]{:S(2)}) %collective-permute-start.6) | collective-permute-done | bytes 524320 | tf_op jit(solution)/shard_map/ppermute | solution.py:15
  110.7 13.2 collective-permute-done.3
  132.9 13.5 collective-permute-done.9
  151.4 17.4 %collective-permute-done.15 = bf16[1024,512]{0,1:T(8,128)(2,1)S(1)} collective-permute-done((bf16[1024,512]{0,1:T(8,128)(2,1)S(1)}, bf16[1024,512]{0,1:T(8,128)(2,1)S(1)}, u32[]{:S(2)}, u32[]{:S(2)}) %collective-permute-start.15) | collective-permute-done | bytes 1048608 | tf_op jit(solution)/shard_map/ppermute | solution.py:15
  168.8 8.6 fusion.112
  177.4 8.1 fusion.1
  185.5 28.3 %collective-permute-done.5 = bf16[1024,512]{0,1:T(8,128)(2,1)} collective-permute-done((bf16[1024,512]{0,1:T(8,128)(2,1)}, bf16[1024,512]{0,1:T(8,128)(2,1)}, u32[]{:S(2)}, u32[]{:S(2)}) %collective-permute-start.5) | collective-permute-done | bytes 1048608 | tf_op jit(solution)/shard_map/ppermute | solution.py:15
  213.9 8.3 fusion.30
  233.7 16.4 %collective-permute-done.18 = bf16[256,2048]{1,0:T(8,128)(2,1)S(1)} collective-permute-done((bf16[256,2048]{1,0:T(8,128)(2,1)S(1)}, bf16[256,2048]{1,0:T(8,128)(2,1)S(1)}, u32[]{:S(2)}, u32[]{:S(2)}) %collective-permute-start.18) | collective-permute-done | bytes 1048608 | tf_op jit(solution)/shard_map/ppermute | solution.py:15
  254.3 80.8 %collective-permute-done.19 = bf16[128,2048]{1,0:T(8,128)(2,1)S(1)} collective-permute-done((bf16[128,2048]{1,0:T(8,128)(2,1)S(1)}, bf16[128,2048]{1,0:T(8,128)(2,1)S(1)}, u32[]{:S(2)}, u32[]{:S(2)}) %collective-permute-start.19) | collective-permute-done | bytes 524320 | tf_op jit(solution)/shard_map/ppermute | solution.py:15
  338.4 11.0 collective-permute-done.20
  356.1 5.9 collective-permute-done.28
  371.8 26.3 %multiply_convert_fusion.1 = (bf16[512,2048]{1,0:T(8,128)(2,1)}, f32[512,2048]{1,0:T(8,128)}, f32[512,2048]{1,0:T(8,128)}) fusion(bf16[2048,1024]{1,0:T(8,128)(2,1)} %copy-done.24, bf16[2048,1024]{1,0:T(8,128)(2,1)} %copy-done.80, pred[]{:T(512)S(6)} %eq.154, bf16[256,2048]{1,0:T(8,128)(2,1)} %copy-done.44, bf16[256,2048]{1,0:T(8,128)(2,1)} %collective-permute-done.21, ...), kind=kOutput, calls=%fused_computation.37 | convolution fusion | flops 4410310656 | bytes 20971522 | tf_op jit(solution)/shard_map/dot_general | solution.py:218
  398.1 52.9 %collective-permute-done.25 = bf16[1024,2048]{1,0:T(8,128)(2,1)} collective-permute-done((bf16[1024,2048]{1,0:T(8,128)(2,1)}, bf16[1024,2048]{1,0:T(8,128)(2,1)}, u32[]{:S(2)}, u32[]{:S(2)}) %collective-permute-start.25) | collective-permute-done | bytes 4194336 | tf_op jit(solution)/shard_map/ppermute | solution.py:15
  451.0 20.3 %add_convert_fusion.2 = bf16[512,2048]{1,0:T(8,128)(2,1)} fusion(f32[512,2048]{1,0:T(8,128)} %get-tuple-element.156, f32[512,2048]{1,0:T(8,128)} %get-tuple-element.171, bf16[1024,2048]{1,0:T(8,128)(2,1)} %maximum_select_fusion.3, bf16[1024,2048]{1,0:T(8,128)(2,1)} %collective-permute-done.25, pred[]{:T(512)S(6)} %eq.154, ...), kind=kOutput, calls=%fused_computation.36 | convolution fusion | flops 4356833280 | bytes 20971522 | tf_op jit(solution)/shard_map/dot_general | solution.py:55
  471.3 10.6 fusion.27
  482.2 10.2 fusion.26
  494.3 7.0 fusion.54
  501.3 34.4 %collective-permute-done.30 = bf16[256,2048]{1,0:T(8,128)(2,1)} collective-permute-done((bf16[256,2048]{1,0:T(8,128)(2,1)S(1)}, bf16[256,2048]{1,0:T(8,128)(2,1)}, u32[]{:S(2)}, u32[]{:S(2)}) %collective-permute-start.30) | collective-permute-done | bytes 1048608 | tf_op jit(solution)/shard_map/ppermute | solution.py:15
  549.5 10.4 collective-permute-done.27
  572.9 7.1 fusion.53
  598.7 14.3 %multiply_reduce_fusion = (f32[4,512]{1,0:T(4,128)S(1)}, f32[4,512,2048]{2,1,0:T(8,128)}) fusion(f32[4,512,2048]{2,1,0:T(8,128)} %get-tuple-element.170, f32[4,512]{1,0:T(4,128)S(1)} %log_add_fusion, bf16[512,4,128]{0,2,1:T(8,128)(2,1)S(1)} %bitcast.140, bf16[1024,4,128]{0,2,1:T(8,128)(2,1)S(1)} %copy-done.29, bf16[1024,4,128]{0,2,1:T(8,128)(2,1)} %bitcast.5, ...), kind=kOutput, calls=%fused_computation.3 | convolution fusion | flops 1095759872 | bytes 36192256 | tf_op jit(solution)/shard_map/while/body/eval_jaxpr/qhd,khd->hqk/dot_general | solution.py:252
  613.1 15.9 %multiply_convert_fusion = bf16[4,512,2048]{2,1,0:T(8,128)(2,1)} fusion(f32[4,512,2048]{2,1,0:T(8,128)} %get-tuple-element.173, f32[4,512,2048]{2,1,0:T(8,128)} %get-tuple-element.170, f32[4,512]{1,0:T(4,128)S(1)} %get-tuple-element.172, f32[4,512]{1,0:T(4,128)S(1)} %log_add_fusion), kind=kLoop, calls=%fused_computation.2 | loop fusion | flops 16777216 | bytes 41959424 | tf_op jit(solution)/shard_map/while/body/eval_jaxpr/convert_element_type | solution.py:256
  629.0 6.3 fusion.29
  651.4 121.1 %collective-permute-done.46 = bf16[256,2048]{1,0:T(8,128)(2,1)S(1)} collective-permute-done((bf16[256,2048]{1,0:T(8,128)(2,1)S(1)}, bf16[256,2048]{1,0:T(8,128)(2,1)S(1)}, u32[]{:S(2)}, u32[]{:S(2)}) %collective-permute-start.46) | collective-permute-done | bytes 1048608 | tf_op jit(solution)/shard_map/ppermute | solution.py:15
  774.2 20.8 %collective-permute-done.36 = bf16[1024,512]{0,1:T(8,128)(2,1)S(1)} collective-permute-done((bf16[1024,512]{0,1:T(8,128)(2,1)S(1)}, bf16[1024,512]{0,1:T(8,128)(2,1)S(1)}, u32[]{:S(2)}, u32[]{:S(2)}) %collective-permute-start.36) | collective-permute-done | bytes 1048608 | tf_op jit(solution)/shard_map/ppermute | solution.py:15
  795.0 12.9 collective-permute-start.47
  809.3 8.2 collective-permute-done.34
  817.5 12.9 collective-permute-start.37
  833.0 7.0 collective-permute-done.40
  840.0 6.7 collective-permute-start.35
  897.2 16.3 %collective-permute-done.42 = bf16[2048,256]{1,0:T(8,128)(2,1)} collective-permute-done((bf16[2048,256]{1,0:T(8,128)(2,1)}, bf16[2048,256]{1,0:T(8,128)(2,1)}, u32[]{:S(2)}, u32[]{:S(2)}) %collective-permute-start.42) | collective-permute-done | bytes 1048608 | tf_op jit(solution)/shard_map/ppermute | solution.py:15
  917.7 11.7 convert_add_fusion
  936.7 6.7 add_convert_fusion.1
  943.4 18.8 %collective-permute-done.38 = bf16[256,6144]{1,0:T(8,128)(2,1)} collective-permute-done((bf16[256,6144]{1,0:T(8,128)(2,1)}, bf16[256,6144]{1,0:T(8,128)(2,1)}, u32[]{:S(2)}, u32[]{:S(2)}) %collective-permute-start.38) | collective-permute-done | bytes 3145760 | tf_op jit(solution)/shard_map/ppermute | solution.py:15
  962.2 7.4 convert_add_fusion.2
  976.9 29.3 %reduce-scatter.7.cloned.1.call-done = bf16[256,128]{1,0:T(8,128)(2,1)} async-done(((bf16[2048,128]{1,0:T(8,128)(2,1)}), bf16[256,128]{1,0:T(8,128)(2,1)}) %reduce-scatter.7.cloned.1.call-update) | async-done | bytes 65552 | tf_op jit(solution)/shard_map/reduce_scatter | solution.py:323
  1007.8 6.0 add_convert_fusion
  1014.0 65.8 %reduce-scatter.11.cloned.1.call-done = bf16[256,128]{1,0:T(8,128)(2,1)} async-done(((bf16[2048,128]{1,0:T(8,128)(2,1)}), bf16[256,128]{1,0:T(8,128)(2,1)}) %reduce-scatter.11.cloned.1.call-update) | async-done | bytes 65552 | tf_op jit(solution)/shard_map/reduce_scatter | solution.py:329
  1081.3 71.9 %reduce-scatter.9.cloned.1.call-done = bf16[256,128]{1,0:T(8,128)(2,1)} async-done(((bf16[2048,128]{1,0:T(8,128)(2,1)}), bf16[256,128]{1,0:T(8,128)(2,1)}) %reduce-scatter.9.cloned.1.call-update) | async-done | bytes 65552 | tf_op jit(solution)/shard_map/reduce_scatter | solution.py:326
  1164.7 17.9 %fusion.113 = (f32[4,17]{1,0:T(4,128)S(1)}, f32[128,4,17]{2,1,0:T(4,128)S(1)}) fusion(bf16[17,128,2048]{2,1,0:T(8,128)(2,1)S(1)} %bitcast.136, f32[128,2048,4]{1,0,2:T(8,128)S(1)} %add_bitcast_fusion), kind=kOutput, calls=%fused_computation.270 | convolution fusion | flops 213918144 | bytes 13142288 | tf_op jit(solution)/shard_map/transpose(jvp(tkj,jtd->ktd))/dot_general | solution.py:35
  1190.6 25.6 %fusion = bf16[17,128,2048]{2,0,1:T(8,128)(2,1)} fusion(f32[1,128,2048]{2,0,1:T(1,128)S(1)} %broadcast_in_dim.111, f32[128,4,17]{2,1,0:T(4,128)S(1)} %copy-done.33, f32[128,2048,4]{1,0,2:T(8,128)} %copy-done.25), kind=kOutput, calls=%fused_computation.1 | convolution fusion | flops 222822400 | bytes 14190592 | tf_op jit(solution)/shard_map/transpose(jvp(tkj,jtd->ktd))/dot_general | solution.py:35
  1216.2 13.6 %copy.76 = bf16[17,128,2048]{2,1,0:T(8,128)(2,1)} copy(bf16[17,128,2048]{2,0,1:T(8,128)(2,1)} %fusion) | data formatting | bytes 17825792
  1230.1 69.4 %all-reduce.5 = (f32[2048]{0:T(1024)}, f32[68,68]{1,0:T(8,128)}, f32[68]{0:T(128)}, f32[2048]{0:T(1024)}, f32[2048]{0:T(1024)}, /*index=5*/f32[2048]{0:T(1024)}, f32[2048]{0:T(1024)}) all-reduce(f32[2048]{0:T(1024)S(1)} %get-tuple-element.133, f32[68,68]{1,0:T(8,128)S(1)} %fusion.72, ...), channel_id=1, replica_groups=mesh['dp'=8,'tensor'=16] {'dp','tensor'}, use_global_device_ids=true, to_apply=%region_17.18 | all-reduce | flops 14932 | bytes 119456 | tf_op jit(solution)/shard_map/psum | solution.py:309
  1301.3 8.9 reduce-scatter.17.cloned.1.call-done
  1312.0 27.4 %all-reduce.8.cloned.1.call-done = f32[2048,68]{0,1:T(8,128)} async-done(((f32[2048,68]{0,1:T(8,128)}), f32[2048,68]{0,1:T(8,128)}) %all-reduce.8.cloned.1.call-update) | async-done | bytes 557072 | tf_op jit(solution)/shard_map/psum | solution.py:309
  (440 shorter events, 262.0 us)
Async XLA Ops:
  8.0 967.4 %reduce-scatter.13.cloned.1.call-start = ((), (), s32[]{:S(2)}) async-start(), calls=%async_computation.10 | async-start | bytes 589824 | tf_op jit(solution)/shard_map/reduce_scatter | solution.py:332
  8.1 68.1 %collective-permute-start.8 = (bf16[2048,128]{1,0:T(8,128)(2,1)}, bf16[2048,128]{1,0:T(8,128)(2,1)}, u32[]{:S(2)}, u32[]{:S(2)}) collective-permute-start(bf16[2048,128]{1,0:T(8,128)(2,1)} %param.28), channel_id=1, source_target_pairs={{0,1},{1,0},{2,3},{3,2},{4,5},{5,4},{6,7},{7,6},{8,9},{9,8},{10,11... | collective-permute-start | bytes 1572872 | tf_op jit(solution)/shard_map/ppermute | solution.py:15
  9.6 37.6 %collective-permute-start.12 = (bf16[2048,128]{1,0:T(8,128)(2,1)}, bf16[2048,128]{1,0:T(8,128)(2,1)}, u32[]{:S(2)}, u32[]{:S(2)}) collective-permute-start(bf16[2048,128]{1,0:T(8,128)(2,1)} %param.29), channel_id=1, source_target_pairs={{0,1},{1,0},{2,3},{3,2},{4,5},{5,4},{6,7},{7,6},{8,9},{9,8},{10,11... | collective-permute-start | bytes 1572872 | tf_op jit(solution)/shard_map/ppermute | solution.py:15
  9.7 61.6 %collective-permute-start.2 = (bf16[2048,128]{1,0:T(8,128)(2,1)}, bf16[2048,128]{1,0:T(8,128)(2,1)}, u32[]{:S(2)}, u32[]{:S(2)}) collective-permute-start(bf16[2048,128]{1,0:T(8,128)(2,1)} %param.30), channel_id=1, source_target_pairs={{0,1},{1,0},{2,3},{3,2},{4,5},{5,4},{6,7},{7,6},{8,9},{9,8},{10,11... | collective-permute-start | bytes 1572872 | tf_op jit(solution)/shard_map/ppermute | solution.py:15
  40.5 37.9 %collective-permute-start = (bf16[128,2048]{1,0:T(8,128)(2,1)S(1)}, bf16[128,2048]{1,0:T(8,128)(2,1)}, u32[]{:S(2)}, u32[]{:S(2)}) collective-permute-start(bf16[128,2048]{1,0:T(8,128)(2,1)S(1)} %multiply_convert_fusion.5), channel_id=1, source_target_pairs={{0,4},{1,5},{2,6},{3,7},{4,0},{5,1},{6,2},{7,3},{8,12},{9,13},{10,... | collective-permute-start | bytes 1572872 | tf_op jit(solution)/shard_map/ppermute | solution.py:15
  44.9 22.5 %collective-permute-start.10 = (bf16[128,2048]{1,0:T(8,128)(2,1)S(1)}, bf16[128,2048]{1,0:T(8,128)(2,1)}, u32[]{:S(2)}, u32[]{:S(2)}) collective-permute-start(bf16[128,2048]{1,0:T(8,128)(2,1)S(1)} %multiply_convert_fusion.3), channel_id=1, source_target_pairs={{0,4},{1,5},{2,6},{3,7},{4,0},{5,1},{6,2},{7,3},{8,12},{9,13},{10,... | collective-permute-start | bytes 1572872 | tf_op jit(solution)/shard_map/ppermute | solution.py:15
  50.0 52.6 %collective-permute-start.13 = (bf16[2048,256]{1,0:T(8,128)(2,1)}, bf16[2048,256]{1,0:T(8,128)(2,1)}, u32[]{:S(2)}, u32[]{:S(2)}) collective-permute-start(bf16[2048,256]{1,0:T(8,128)(2,1)} %maximum_select_fusion.29), channel_id=1, source_target_pairs={{0,2},{1,3},{2,0},{3,1},{4,6},{5,7},{6,4},{7,5},{8,10},{9,11},{10,... | collective-permute-start | bytes 3145736 | tf_op jit(solution)/shard_map/ppermute | solution.py:15
  70.0 32.9 %collective-permute-start.11 = (bf16[256,2048]{1,0:T(8,128)(2,1)}, bf16[256,2048]{1,0:T(8,128)(2,1)}, u32[]{:S(2)}, u32[]{:S(2)}) collective-permute-start(bf16[256,2048]{1,0:T(8,128)(2,1)} %maximum_select_fusion.28), channel_id=1, source_target_pairs={{0,8},{1,9},{2,10},{3,11},{4,12},{5,13},{6,14},{7,15},{8,0},{9,1},... | collective-permute-start | bytes 3145736 | tf_op jit(solution)/shard_map/ppermute | solution.py:15
  71.3 29.7 %collective-permute-start.6 = (bf16[128,2048]{1,0:T(8,128)(2,1)S(1)}, bf16[128,2048]{1,0:T(8,128)(2,1)S(1)}, u32[]{:S(2)}, u32[]{:S(2)}) collective-permute-start(bf16[128,2048]{1,0:T(8,128)(2,1)S(1)} %multiply_convert_fusion.4), channel_id=1, source_target_pairs={{0,4},{1,5},{2,6},{3,7},{4,0},{5,1},{6,2},{7,3},{8,12},{9,13},{10,... | collective-permute-start | bytes 1572872 | tf_op jit(solution)/shard_map/ppermute | solution.py:15
  76.1 47.7 %collective-permute-start.3 = (bf16[2048,256]{1,0:T(8,128)(2,1)S(1)}, bf16[2048,256]{1,0:T(8,128)(2,1)S(1)}, u32[]{:S(2)}, u32[]{:S(2)}) collective-permute-start(bf16[2048,256]{1,0:T(8,128)(2,1)S(1)} %maximum_select_fusion.23), channel_id=1, source_target_pairs={{0,2},{1,3},{2,0},{3,1},{4,6},{5,7},{6,4},{7,5},{8,10},{9,11},{10,... | collective-permute-start | bytes 3145736 | tf_op jit(solution)/shard_map/ppermute | solution.py:15
  78.5 67.9 %collective-permute-start.9 = (bf16[2048,256]{1,0:T(8,128)(2,1)S(1)}, bf16[2048,256]{1,0:T(8,128)(2,1)S(1)}, u32[]{:S(2)}, u32[]{:S(2)}) collective-permute-start(bf16[2048,256]{1,0:T(8,128)(2,1)S(1)} %maximum_select_fusion.27), channel_id=1, source_target_pairs={{0,2},{1,3},{2,0},{3,1},{4,6},{5,7},{6,4},{7,5},{8,10},{9,11},{10,... | collective-permute-start | bytes 3145736 | tf_op jit(solution)/shard_map/ppermute | solution.py:15
  101.0 24.2 %collective-permute-start.1 = (bf16[256,2048]{1,0:T(8,128)(2,1)S(1)}, bf16[256,2048]{1,0:T(8,128)(2,1)S(1)}, u32[]{:S(2)}, u32[]{:S(2)}) collective-permute-start(bf16[256,2048]{1,0:T(8,128)(2,1)S(1)} %maximum_select_fusion.22), channel_id=1, source_target_pairs={{0,8},{1,9},{2,10},{3,11},{4,12},{5,13},{6,14},{7,15},{8,0},{9,1},... | collective-permute-start | bytes 3145736 | tf_op jit(solution)/shard_map/ppermute | solution.py:15
  102.6 45.0 %collective-permute-start.7 = (bf16[256,2048]{1,0:T(8,128)(2,1)S(1)}, bf16[256,2048]{1,0:T(8,128)(2,1)S(1)}, u32[]{:S(2)}, u32[]{:S(2)}) collective-permute-start(bf16[256,2048]{1,0:T(8,128)(2,1)S(1)} %maximum_select_fusion.26), channel_id=1, source_target_pairs={{0,8},{1,9},{2,10},{3,11},{4,12},{5,13},{6,14},{7,15},{8,0},{9,1},... | collective-permute-start | bytes 3145736 | tf_op jit(solution)/shard_map/ppermute | solution.py:15
  125.2 102.2 %collective-permute-start.22 = (bf16[2048,512]{1,0:T(8,128)(2,1)}, bf16[2048,512]{1,0:T(8,128)(2,1)}, u32[]{:S(2)}, u32[]{:S(2)}) collective-permute-start(bf16[2048,512]{1,0:T(8,128)(2,1)} %param.32), channel_id=1, source_target_pairs={{0,1},{1,0},{2,3},{3,2},{4,5},{5,4},{6,7},{7,6},{8,9},{9,8},{10,11... | collective-permute-start | bytes 6291464 | tf_op jit(solution)/shard_map/ppermute | solution.py:15
  130.2 38.6 %collective-permute-start.15 = (bf16[1024,512]{0,1:T(8,128)(2,1)S(1)}, bf16[1024,512]{0,1:T(8,128)(2,1)S(1)}, u32[]{:S(2)}, u32[]{:S(2)}) collective-permute-start(bf16[1024,512]{0,1:T(8,128)(2,1)S(1)} %maximum_select_fusion.30), channel_id=1, source_target_pairs={{0,2},{1,3},{2,0},{3,1},{4,6},{5,7},{6,4},{7,5},{8,10},{9,11},{10,... | collective-permute-start | bytes 3145736 | tf_op jit(solution)/shard_map/ppermute | solution.py:15
  146.4 75.9 %collective-permute-start.17 = (bf16[256,2048]{1,0:T(8,128)(2,1)}, bf16[256,2048]{1,0:T(8,128)(2,1)}, u32[]{:S(2)}, u32[]{:S(2)}) collective-permute-start(bf16[256,2048]{1,0:T(8,128)(2,1)} %maximum_select_fusion.32), channel_id=1, source_target_pairs={{0,2},{1,3},{2,0},{3,1},{4,6},{5,7},{6,4},{7,5},{8,10},{9,11},{10,... | collective-permute-start | bytes 3145736 | tf_op jit(solution)/shard_map/ppermute | solution.py:15
  150.2 63.7 %collective-permute-start.5 = (bf16[1024,512]{0,1:T(8,128)(2,1)}, bf16[1024,512]{0,1:T(8,128)(2,1)}, u32[]{:S(2)}, u32[]{:S(2)}) collective-permute-start(bf16[1024,512]{0,1:T(8,128)(2,1)} %maximum_select_fusion.24), channel_id=1, source_target_pairs={{0,2},{1,3},{2,0},{3,1},{4,6},{5,7},{6,4},{7,5},{8,10},{9,11},{10,... | collective-permute-start | bytes 3145736 | tf_op jit(solution)/shard_map/ppermute | solution.py:15
  226.1 23.9 %collective-permute-start.18 = (bf16[256,2048]{1,0:T(8,128)(2,1)S(1)}, bf16[256,2048]{1,0:T(8,128)(2,1)S(1)}, u32[]{:S(2)}, u32[]{:S(2)}) collective-permute-start(bf16[256,2048]{1,0:T(8,128)(2,1)S(1)} %select_convert_fusion.14), channel_id=1, source_target_pairs={{0,8},{1,9},{2,10},{3,11},{4,12},{5,13},{6,14},{7,15},{8,0},{9,1},... | collective-permute-start | bytes 3145736 | tf_op jit(solution)/shard_map/ppermute | solution.py:15
  232.5 131.4 %collective-permute-start.23 = (bf16[2048,1024]{1,0:T(8,128)(2,1)S(1)}, bf16[2048,1024]{1,0:T(8,128)(2,1)S(1)}, u32[]{:S(2)}, u32[]{:S(2)}) collective-permute-start(bf16[2048,1024]{1,0:T(8,128)(2,1)S(1)} %maximum_select_fusion.2), channel_id=1, source_target_pairs={{0,2},{1,3},{2,0},{3,1},{4,6},{5,7},{6,4},{7,5},{8,10},{9,11},{10,... | collective-permute-start | bytes 12582920 | tf_op jit(solution)/shard_map/ppermute | solution.py:15
  250.6 84.5 %collective-permute-start.19 = (bf16[128,2048]{1,0:T(8,128)(2,1)S(1)}, bf16[128,2048]{1,0:T(8,128)(2,1)S(1)}, u32[]{:S(2)}, u32[]{:S(2)}) collective-permute-start(bf16[128,2048]{1,0:T(8,128)(2,1)S(1)} %select_convert_fusion.23), channel_id=1, source_target_pairs={{0,4},{1,5},{2,6},{3,7},{4,0},{5,1},{6,2},{7,3},{8,12},{9,13},{10,... | collective-permute-start | bytes 1572872 | tf_op jit(solution)/shard_map/ppermute | solution.py:15
  252.2 99.6 %collective-permute-start.24 = (bf16[512,2048]{1,0:T(8,128)(2,1)S(1)}, bf16[512,2048]{1,0:T(8,128)(2,1)S(1)}, u32[]{:S(2)}, u32[]{:S(2)}) collective-permute-start(bf16[512,2048]{1,0:T(8,128)(2,1)S(1)} %copy-done.31), channel_id=1, source_target_pairs={{0,1},{1,0},{2,3},{3,2},{4,5},{5,4},{6,7},{7,6},{8,9},{9,8},{10,11... | collective-permute-start | bytes 6291464 | tf_op jit(solution)/shard_map/ppermute | solution.py:15
  349.7 22.1 %collective-permute-start.21 = (bf16[256,2048]{1,0:T(8,128)(2,1)S(1)}, bf16[256,2048]{1,0:T(8,128)(2,1)}, u32[]{:S(2)}, u32[]{:S(2)}) collective-permute-start(bf16[256,2048]{1,0:T(8,128)(2,1)S(1)} %maximum_select_fusion.33), channel_id=1, source_target_pairs={{0,8},{1,9},{2,10},{3,11},{4,12},{5,13},{6,14},{7,15},{8,0},{9,1},... | collective-permute-start | bytes 3145736 | tf_op jit(solution)/shard_map/ppermute | solution.py:15
  355.6 95.4 %collective-permute-start.25 = (bf16[1024,2048]{1,0:T(8,128)(2,1)}, bf16[1024,2048]{1,0:T(8,128)(2,1)}, u32[]{:S(2)}, u32[]{:S(2)}) collective-permute-start(bf16[1024,2048]{1,0:T(8,128)(2,1)} %maximum_select_fusion.3), channel_id=1, source_target_pairs={{0,2},{1,3},{2,0},{3,1},{4,6},{5,7},{6,4},{7,5},{8,10},{9,11},{10,... | collective-permute-start | bytes 12582920 | tf_op jit(solution)/shard_map/ppermute | solution.py:15
  362.2 35.9 %collective-permute-start.29 = (bf16[256,2048]{1,0:T(8,128)(2,1)S(1)}, bf16[256,2048]{1,0:T(8,128)(2,1)}, u32[]{:S(2)}, u32[]{:S(2)}) collective-permute-start(bf16[256,2048]{1,0:T(8,128)(2,1)S(1)} %maximum_select_fusion.34), channel_id=1, source_target_pairs={{0,8},{1,9},{2,10},{3,11},{4,12},{5,13},{6,14},{7,15},{8,0},{9,1},... | collective-permute-start | bytes 3145736 | tf_op jit(solution)/shard_map/ppermute | solution.py:15
  492.6 47.8 %collective-permute-start.26 = (bf16[256,2048]{1,0:T(8,128)(2,1)S(1)}, bf16[256,2048]{1,0:T(8,128)(2,1)}, u32[]{:S(2)}, u32[]{:S(2)}) collective-permute-start(bf16[256,2048]{1,0:T(8,128)(2,1)S(1)} %select_convert_fusion.13), channel_id=1, source_target_pairs={{0,8},{1,9},{2,10},{3,11},{4,12},{5,13},{6,14},{7,15},{8,0},{9,1},... | collective-permute-start | bytes 3145736 | tf_op jit(solution)/shard_map/ppermute | solution.py:15
  493.9 41.8 %collective-permute-start.30 = (bf16[256,2048]{1,0:T(8,128)(2,1)S(1)}, bf16[256,2048]{1,0:T(8,128)(2,1)}, u32[]{:S(2)}, u32[]{:S(2)}) collective-permute-start(bf16[256,2048]{1,0:T(8,128)(2,1)S(1)} %select_convert_fusion.12), channel_id=1, source_target_pairs={{0,8},{1,9},{2,10},{3,11},{4,12},{5,13},{6,14},{7,15},{8,0},{9,1},... | collective-permute-start | bytes 3145736 | tf_op jit(solution)/shard_map/ppermute | solution.py:15
  565.6 281.5 %collective-permute-start.48 = (bf16[2048,1024]{1,0:T(8,128)(2,1)}, bf16[2048,1024]{1,0:T(8,128)(2,1)}, u32[]{:S(2)}, u32[]{:S(2)}) collective-permute-start(bf16[2048,1024]{1,0:T(8,128)(2,1)} %select_convert_fusion.1), channel_id=1, source_target_pairs={{0,2},{1,3},{2,0},{3,1},{4,6},{5,7},{6,4},{7,5},{8,10},{9,11},{10,... | collective-permute-start | bytes 12582920 | tf_op jit(solution)/shard_map/ppermute | solution.py:15
  588.3 329.4 %collective-permute-start.50 = (bf16[1024,2048]{1,0:T(8,128)(2,1)}, bf16[1024,2048]{1,0:T(8,128)(2,1)}, u32[]{:S(2)}, u32[]{:S(2)}) collective-permute-start(bf16[1024,2048]{1,0:T(8,128)(2,1)} %select_convert_fusion), channel_id=1, source_target_pairs={{0,2},{1,3},{2,0},{3,1},{4,6},{5,7},{6,4},{7,5},{8,10},{9,11},{10,... | collective-permute-start | bytes 12582920 | tf_op jit(solution)/shard_map/ppermute | solution.py:15
  642.1 130.5 %collective-permute-start.46 = (bf16[256,2048]{1,0:T(8,128)(2,1)S(1)}, bf16[256,2048]{1,0:T(8,128)(2,1)S(1)}, u32[]{:S(2)}, u32[]{:S(2)}) collective-permute-start(bf16[256,2048]{1,0:T(8,128)(2,1)S(1)} %select_convert_fusion.6), channel_id=1, source_target_pairs={{0,2},{1,3},{2,0},{3,1},{4,6},{5,7},{6,4},{7,5},{8,10},{9,11},{10,... | collective-permute-start | bytes 3145736 | tf_op jit(solution)/shard_map/ppermute | solution.py:15
  643.4 151.7 %collective-permute-start.36 = (bf16[1024,512]{0,1:T(8,128)(2,1)S(1)}, bf16[1024,512]{0,1:T(8,128)(2,1)S(1)}, u32[]{:S(2)}, u32[]{:S(2)}) collective-permute-start(bf16[1024,512]{0,1:T(8,128)(2,1)S(1)} %bitcast.146), channel_id=1, source_target_pairs={{0,2},{1,3},{2,0},{3,1},{4,6},{5,7},{6,4},{7,5},{8,10},{9,11},{10,... | collective-permute-start | bytes 3145736 | tf_op jit(solution)/shard_map/ppermute | solution.py:15
  644.1 173.4 %collective-permute-start.34 = (bf16[1024,512]{0,1:T(8,128)(2,1)S(1)}, bf16[1024,512]{0,1:T(8,128)(2,1)S(1)}, u32[]{:S(2)}, u32[]{:S(2)}) collective-permute-start(bf16[1024,512]{0,1:T(8,128)(2,1)S(1)} %bitcast.145), channel_id=1, source_target_pairs={{0,2},{1,3},{2,0},{3,1},{4,6},{5,7},{6,4},{7,5},{8,10},{9,11},{10,... | collective-permute-start | bytes 3145736 | tf_op jit(solution)/shard_map/ppermute | solution.py:15
  772.6 67.4 %collective-permute-start.40 = (bf16[2048,256]{1,0:T(8,128)(2,1)S(1)}, bf16[2048,256]{1,0:T(8,128)(2,1)S(1)}, u32[]{:S(2)}, u32[]{:S(2)}) collective-permute-start(bf16[2048,256]{1,0:T(8,128)(2,1)S(1)} %select_convert_fusion.9), channel_id=1, source_target_pairs={{0,2},{1,3},{2,0},{3,1},{4,6},{5,7},{6,4},{7,5},{8,10},{9,11},{10,... | collective-permute-start | bytes 3145736 | tf_op jit(solution)/shard_map/ppermute | solution.py:15
  795.0 63.3 %collective-permute-start.47 = (bf16[128,2048]{1,0:T(8,128)(2,1)}, bf16[128,2048]{1,0:T(8,128)(2,1)}, u32[]{:S(2)}, u32[]{:S(2)}) collective-permute-start(bf16[128,2048]{1,0:T(8,128)(2,1)} %select_convert_fusion.15), channel_id=1, source_target_pairs={{0,1},{1,0},{2,3},{3,2},{4,5},{5,4},{6,7},{7,6},{8,9},{9,8},{10,11... | collective-permute-start | bytes 1572872 | tf_op jit(solution)/shard_map/ppermute | solution.py:15
  817.5 43.5 %collective-permute-start.37 = (bf16[512,512]{0,1:T(8,128)(2,1)}, bf16[512,512]{0,1:T(8,128)(2,1)}, u32[]{:S(2)}, u32[]{:S(2)}) collective-permute-start(bf16[512,512]{0,1:T(8,128)(2,1)} %select_convert_fusion.19), channel_id=1, source_target_pairs={{0,1},{1,0},{2,3},{3,2},{4,5},{5,4},{6,7},{7,6},{8,9},{9,8},{10,11... | collective-permute-start | bytes 1572872 | tf_op jit(solution)/shard_map/ppermute | solution.py:15
  840.0 27.3 %collective-permute-start.35 = (bf16[512,512]{0,1:T(8,128)(2,1)}, bf16[512,512]{0,1:T(8,128)(2,1)}, u32[]{:S(2)}, u32[]{:S(2)}) collective-permute-start(bf16[512,512]{0,1:T(8,128)(2,1)} %select_convert_fusion.20), channel_id=1, source_target_pairs={{0,1},{1,0},{2,3},{3,2},{4,5},{5,4},{6,7},{7,6},{8,9},{9,8},{10,11... | collective-permute-start | bytes 1572872 | tf_op jit(solution)/shard_map/ppermute | solution.py:15
  848.3 41.2 %collective-permute-start.41 = (bf16[2048,128]{1,0:T(8,128)(2,1)S(1)}, bf16[2048,128]{1,0:T(8,128)(2,1)}, u32[]{:S(2)}, u32[]{:S(2)}) collective-permute-start(bf16[2048,128]{1,0:T(8,128)(2,1)S(1)} %select_convert_fusion.18), channel_id=1, source_target_pairs={{0,1},{1,0},{2,3},{3,2},{4,5},{5,4},{6,7},{7,6},{8,9},{9,8},{10,11... | collective-permute-start | bytes 1572872 | tf_op jit(solution)/shard_map/ppermute | solution.py:15
  858.3 78.3 %collective-permute-start.49 = (bf16[2048,512]{1,0:T(8,128)(2,1)}, bf16[2048,512]{1,0:T(8,128)(2,1)}, u32[]{:S(2)}, u32[]{:S(2)}) collective-permute-start(bf16[2048,512]{1,0:T(8,128)(2,1)} %select_convert_fusion.4), channel_id=1, source_target_pairs={{0,1},{1,0},{2,3},{3,2},{4,5},{5,4},{6,7},{7,6},{8,9},{9,8},{10,11... | collective-permute-start | bytes 6291464 | tf_op jit(solution)/shard_map/ppermute | solution.py:15
  860.9 145.3 %reduce-scatter.7.cloned.1.call-start = ((), (), s32[]{:S(2)}) async-start(), calls=%async_computation.7 | async-start | bytes 589824 | tf_op jit(solution)/shard_map/reduce_scatter | solution.py:323
  866.2 26.7 %collective-permute-start.44 = (bf16[2048,256]{1,0:T(8,128)(2,1)S(1)}, bf16[2048,256]{1,0:T(8,128)(2,1)}, u32[]{:S(2)}, u32[]{:S(2)}) collective-permute-start(bf16[2048,256]{1,0:T(8,128)(2,1)S(1)} %select_convert_fusion.7), channel_id=1, source_target_pairs={{0,2},{1,3},{2,0},{3,1},{4,6},{5,7},{6,4},{7,5},{8,10},{9,11},{10,... | collective-permute-start | bytes 3145736 | tf_op jit(solution)/shard_map/ppermute | solution.py:15
  875.6 38.0 %collective-permute-start.42 = (bf16[2048,256]{1,0:T(8,128)(2,1)}, bf16[2048,256]{1,0:T(8,128)(2,1)}, u32[]{:S(2)}, u32[]{:S(2)}) collective-permute-start(bf16[2048,256]{1,0:T(8,128)(2,1)} %select_convert_fusion.8), channel_id=1, source_target_pairs={{0,2},{1,3},{2,0},{3,1},{4,6},{5,7},{6,4},{7,5},{8,10},{9,11},{10,... | collective-permute-start | bytes 3145736 | tf_op jit(solution)/shard_map/ppermute | solution.py:15
  889.5 72.7 %collective-permute-start.38 = (bf16[256,6144]{1,0:T(8,128)(2,1)}, bf16[256,6144]{1,0:T(8,128)(2,1)}, u32[]{:S(2)}, u32[]{:S(2)}) collective-permute-start(bf16[256,6144]{1,0:T(8,128)(2,1)} %select_convert_fusion.2), channel_id=1, source_target_pairs={{0,8},{1,9},{2,10},{3,11},{4,12},{5,13},{6,14},{7,15},{8,0},{9,1},... | collective-permute-start | bytes 9437192 | tf_op jit(solution)/shard_map/ppermute | solution.py:15
  892.9 186.9 %reduce-scatter.11.cloned.1.call-start = ((), (), s32[]{:S(2)}) async-start(), calls=%async_computation.9 | async-start | bytes 589824 | tf_op jit(solution)/shard_map/reduce_scatter | solution.py:329
  917.7 235.6 %reduce-scatter.9.cloned.1.call-start = ((), (), s32[]{:S(2)}) async-start(), calls=%async_computation.8 | async-start | bytes 589824 | tf_op jit(solution)/shard_map/reduce_scatter | solution.py:326
  931.4 368.1 %reduce-scatter.15.cloned.1.call-start = ((), (), s32[]{:S(2)}) async-start(), calls=%async_computation.11 | async-start | bytes 2359296 | tf_op jit(solution)/shard_map/reduce_scatter | solution.py:335
  936.6 71.1 %collective-permute-start.51 = (bf16[512,2048]{1,0:T(8,128)(2,1)}, bf16[512,2048]{1,0:T(8,128)(2,1)S(1)}, u32[]{:S(2)}, u32[]{:S(2)}) collective-permute-start(bf16[512,2048]{1,0:T(8,128)(2,1)} %select_convert_fusion.3), channel_id=1, source_target_pairs={{0,1},{1,0},{2,3},{3,2},{4,5},{5,4},{6,7},{7,6},{8,9},{9,8},{10,11... | collective-permute-start | bytes 6291464 | tf_op jit(solution)/shard_map/ppermute | solution.py:15
  943.3 366.9 %reduce-scatter.17.cloned.1.call-start = ((), (), s32[]{:S(2)}) async-start(), calls=%async_computation.12 | async-start | bytes 2359296 | tf_op jit(solution)/shard_map/reduce_scatter | solution.py:338
  973.8 181.0 %collective-permute-start.39 = (bf16[128,6144]{1,0:T(8,128)(2,1)}, bf16[128,6144]{1,0:T(8,128)(2,1)}, u32[]{:S(2)}, u32[]{:S(2)}) collective-permute-start(bf16[128,6144]{1,0:T(8,128)(2,1)} %select_convert_fusion.5), channel_id=1, source_target_pairs={{0,4},{1,5},{2,6},{3,7},{4,0},{5,1},{6,2},{7,3},{8,12},{9,13},{10,... | collective-permute-start | bytes 4718600 | tf_op jit(solution)/shard_map/ppermute | solution.py:15
  1013.8 325.6 %all-reduce.8.cloned.1.call-start = ((), (), s32[]{:S(2)}) async-start(), calls=%async_computation.6 | async-start | bytes 1179648 | tf_op jit(solution)/shard_map/psum | solution.py:309
  (116 other events, 1572.8 us)
Sparse Core Ops, SparseCore 0:
  861.0 71.6 reduce-scatter.12
  936.8 69.4 reduce-scatter.6
  1010.8 68.9 reduce-scatter.10
  1083.8 69.4 reduce-scatter.8
  1157.3 74.6 reduce-scatter.14
  1235.9 74.2 reduce-scatter.16
Sparse Core Ops, SparseCore 1:
  1190.6 148.7 all-reduce.7
where the time goes:
time: 1350 us
  waiting for transfers between devices  731 us (54%)
  matrix products  235 us (17%)
  other arithmetic  157 us (12%)
  starting transfers between devices  90.5 us (7%)
  blocking collectives  69.4 us (5%)
  local copies, waits for them, and re-layouts  49.2 us (4%)
  between operations  17.8 us (1%)
    ppermute x52, waiting for transfers between devices, swapped(): lax.ppermute(x, axis, [(i, i ^ 1 << bit) for i in range(lax.axis_size(axi...  528 us
    ppermute x52, starting transfers between devices, swapped(): lax.ppermute(x, axis, [(i, i ^ 1 << bit) for i in range(lax.axis_size(axi...  90.1 us
    reduce_scatter x1, waiting for transfers between devices, on_device(): lax.psum_scatter(grad_w_key.astype(jnp.bfloat16), 'dp', scatter_dimension...  71.9 us
    psum x1, blocking collectives, on_device(): lax.psum((front_grads[1], front_grads[2], front_grads[3], front_grads[4],...  69.4 us
    reduce_scatter x1, waiting for transfers between devices, on_device(): lax.psum_scatter(grad_w_value.astype(jnp.bfloat16), 'dp', scatter_dimensi...  65.8 us
    dot_general x3, matrix products, front_part(): jnp.einsum('tkj,jtd->ktd', mixing, history_float, precision=PRECISE)  63.3 us
    unnamed x212, local copies, waits for them, and re-layouts  44.7 us
    dot_general x6, matrix products, across_cols(): lax.dot_general(left_side, right_side, (((1,), (1,)), ((), ())), preferre...  43.8 us
  transfers between devices with their start and end apart: 59, of which 27 were waited for; matrix products, arithmetic and copies ran while one was open for 27% of the time, Pallas kernels for 0%

commit v1 on v0

--- a/solution.py
+++ b/solution.py
@@ -306,19 +306,18 @@
         )
     )
     grad_history = front_grads[0].astype(jnp.bfloat16)
-    small_sums = lax.psum(
-        (
-            front_grads[1],
-            front_grads[2],
-            front_grads[3],
-            front_grads[4],
-            front_grads[5],
-            front_grads[6],
-            front_grads[7],
-            grad_gain_mlp,
-        ),
-        ("dp", "tensor"),
-    )
+    base_x = (
+        front_grads[1],
+        front_grads[2],
+        front_grads[3],
+        front_grads[4],
+        front_grads[5],
+        front_grads[6],
+        front_grads[7],
+        grad_gain_mlp,
+    )
+    all_values = jax.lax.psum(base_x, "tensor")
+    small_sums = jax.lax.psum(all_values, "dp")
     sum_query, sum_key, sum_value, sum_output, sum_expand, sum_reduce = (
         lax.psum_scatter(
             grad_w_query.astype(jnp.bfloat16), "dp", scatter_dimension=0, tiled=True

time: 1350 us -> 1410 us (1.044)
  waiting for transfers between devices: 731 us -> 771 us
  blocking collectives: 69.4 us -> 87.1 us
    psum x1 -> x2, waiting for transfers between devices: 27.4 us -> 82.1 us  [the longest x1 82.1 us: on_device(): small_sums = jax.lax.psum(all_values, 'dp')]
    ppermute x52, waiting for transfers between devices: 528 us -> 577 us  [swapped(): lax.ppermute(x, axis, [(i, i ^ 1 << bit) for i in range(lax.axis_size(axi...]
    reduce_scatter x1, waiting for transfers between devices: 65.8 us -> 17.3 us  [on_device(): lax.psum_scatter(grad_w_value.astype(jnp.bfloat16), 'dp', scatter_dimensi...]
    reduce_scatter x1, waiting for transfers between devices: 29.3 us -> 0.01 us  [on_device(): lax.psum_scatter(grad_w_query.astype(jnp.bfloat16), 'dp', scatter_dimensi...]
    psum x1 -> x2, blocking collectives: 69.4 us -> 87.1 us  [the longest x1 52.2 us: on_device(): all_values = jax.lax.psum(base_x, 'tensor')]
    unnamed x212 -> x204, local copies, waits for them, and re-layouts: 44.7 us -> 36.6 us
  transfers between devices with their start and end apart: 59 -> 60, of which waited for: 27 -> 29; matrix products, arithmetic and copies ran while one was open for 27% -> 26% of each run, Pallas kernels for 0% -> 0%
where the time goes in v1:
time: 1410 us; the launch traced here: 1400 us
  waiting for transfers between devices  771 us (55%)
  matrix products  236 us (17%)
  other arithmetic  151 us (11%)
  starting transfers between devices  93.7 us (7%)
  blocking collectives  87.1 us (6%)
  local copies, waits for them, and re-layouts  41 us (3%)
  between operations  17.7 us (1%)
    ppermute x52, waiting for transfers between devices, swapped(): lax.ppermute(x, axis, [(i, i ^ 1 << bit) for i in range(lax.axis_size(axi...  577 us
    ppermute x52, starting transfers between devices, swapped(): lax.ppermute(x, axis, [(i, i ^ 1 << bit) for i in range(lax.axis_size(axi...  92.9 us
    psum x1, waiting for transfers between devices, on_device(): small_sums = jax.lax.psum(all_values, 'dp')  82.1 us
    reduce_scatter x1, waiting for transfers between devices, on_device(): lax.psum_scatter(grad_w_key.astype(jnp.bfloat16), 'dp', scatter_dimension...  72.7 us
    dot_general x3, matrix products, front_part(): jnp.einsum('tkj,jtd->ktd', mixing, history_float, precision=PRECISE)  63.2 us
    psum x1, blocking collectives, on_device(): all_values = jax.lax.psum(base_x, 'tensor')  52.2 us
    dot_general x6, matrix products, across_cols(): lax.dot_general(left_side, right_side, (((1,), (1,)), ((), ())), preferre...  43.8 us
    add x13, other arithmetic, sum_bits(): keep_half + swapped(send_half.astype(jnp.bfloat16), 'tensor', bit_number)...  38.6 us
  transfers between devices with their start and end apart: 60, of which 29 were waited for; matrix products, arithmetic and copies ran while one was open for 26% of the time, Pallas kernels for 0%

profile of v1, /device:TPU:1, one launch (start us, length us, event | category | flops | bytes accessed | tf_op | source)
XLA Modules:
  0.0 1398.0 jit_solution(2002068263584857788)
XLA Ops:
  16.2 19.8 %fusion.22 = f32[4,128,2048]{2,0,1:T(4,128)S(1)} fusion(f32[128,4,17]{2,1,0:T(4,128)S(1)} %copy.62, bf16[17,128,2048]{2,1,0:T(8,128)(2,1)} %param.17), kind=kOutput, calls=%fused_computation.55 | convolution fusion | flops 213909504 | bytes 13142016 | tf_op jit(solution)/shard_map/jvp(tkj,jtd->ktd)/dot_general | solution.py:35
  51.2 16.2 %collective-permute-done.10 = bf16[128,2048]{1,0:T(8,128)(2,1)} collective-permute-done((bf16[128,2048]{1,0:T(8,128)(2,1)S(1)}, bf16[128,2048]{1,0:T(8,128)(2,1)}, u32[]{:S(2)}, u32[]{:S(2)}) %collective-permute-start.10) | collective-permute-done | bytes 524320 | tf_op jit(solution)/shard_map/ppermute | solution.py:15
  81.2 19.8 %collective-permute-done.6 = bf16[128,2048]{1,0:T(8,128)(2,1)S(1)} collective-permute-done((bf16[128,2048]{1,0:T(8,128)(2,1)S(1)}, bf16[128,2048]{1,0:T(8,128)(2,1)S(1)}, u32[]{:S(2)}, u32[]{:S(2)}) %collective-permute-start.6) | collective-permute-done | bytes 524320 | tf_op jit(solution)/shard_map/ppermute | solution.py:15
  110.6 13.2 collective-permute-done.3
  132.9 13.5 collective-permute-done.9
  151.4 17.4 %collective-permute-done.15 = bf16[1024,512]{0,1:T(8,128)(2,1)S(1)} collective-permute-done((bf16[1024,512]{0,1:T(8,128)(2,1)S(1)}, bf16[1024,512]{0,1:T(8,128)(2,1)S(1)}, u32[]{:S(2)}, u32[]{:S(2)}) %collective-permute-start.15) | collective-permute-done | bytes 1048608 | tf_op jit(solution)/shard_map/ppermute | solution.py:15
  168.8 8.6 fusion.112
  177.4 8.1 fusion.1
  185.5 28.3 %collective-permute-done.5 = bf16[1024,512]{0,1:T(8,128)(2,1)} collective-permute-done((bf16[1024,512]{0,1:T(8,128)(2,1)}, bf16[1024,512]{0,1:T(8,128)(2,1)}, u32[]{:S(2)}, u32[]{:S(2)}) %collective-permute-start.5) | collective-permute-done | bytes 1048608 | tf_op jit(solution)/shard_map/ppermute | solution.py:15
  213.8 8.3 fusion.30
  233.6 16.3 %collective-permute-done.18 = bf16[256,2048]{1,0:T(8,128)(2,1)S(1)} collective-permute-done((bf16[256,2048]{1,0:T(8,128)(2,1)S(1)}, bf16[256,2048]{1,0:T(8,128)(2,1)S(1)}, u32[]{:S(2)}, u32[]{:S(2)}) %collective-permute-start.18) | collective-permute-done | bytes 1048608 | tf_op jit(solution)/shard_map/ppermute | solution.py:15
  254.2 80.9 %collective-permute-done.19 = bf16[128,2048]{1,0:T(8,128)(2,1)S(1)} collective-permute-done((bf16[128,2048]{1,0:T(8,128)(2,1)S(1)}, bf16[128,2048]{1,0:T(8,128)(2,1)S(1)}, u32[]{:S(2)}, u32[]{:S(2)}) %collective-permute-start.19) | collective-permute-done | bytes 524320 | tf_op jit(solution)/shard_map/ppermute | solution.py:15
  338.4 11.0 collective-permute-done.20
  371.8 26.4 %multiply_convert_fusion.1 = (bf16[512,2048]{1,0:T(8,128)(2,1)}, f32[512,2048]{1,0:T(8,128)}, f32[512,2048]{1,0:T(8,128)}) fusion(bf16[2048,1024]{1,0:T(8,128)(2,1)} %copy-done.19, bf16[2048,1024]{1,0:T(8,128)(2,1)} %copy-done.76, pred[]{:T(512)S(6)} %eq.154, bf16[256,2048]{1,0:T(8,128)(2,1)} %copy-done.38, bf16[256,2048]{1,0:T(8,128)(2,1)} %collective-permute-done.21, ...), kind=kOutput, calls=%fused_computation.37 | convolution fusion | flops 4410310656 | bytes 20971522 | tf_op jit(solution)/shard_map/dot_general | solution.py:218
  398.3 52.6 %collective-permute-done.25 = bf16[1024,2048]{1,0:T(8,128)(2,1)} collective-permute-done((bf16[1024,2048]{1,0:T(8,128)(2,1)}, bf16[1024,2048]{1,0:T(8,128)(2,1)}, u32[]{:S(2)}, u32[]{:S(2)}) %collective-permute-start.25) | collective-permute-done | bytes 4194336 | tf_op jit(solution)/shard_map/ppermute | solution.py:15
  450.9 20.4 %add_convert_fusion.2 = bf16[512,2048]{1,0:T(8,128)(2,1)} fusion(f32[512,2048]{1,0:T(8,128)} %get-tuple-element.163, f32[512,2048]{1,0:T(8,128)} %get-tuple-element.178, bf16[1024,2048]{1,0:T(8,128)(2,1)} %maximum_select_fusion.3, bf16[1024,2048]{1,0:T(8,128)(2,1)} %collective-permute-done.25, pred[]{:T(512)S(6)} %eq.154, ...), kind=kOutput, calls=%fused_computation.36 | convolution fusion | flops 4356833280 | bytes 20971522 | tf_op jit(solution)/shard_map/dot_general | solution.py:55
  471.2 10.6 fusion.27
  482.1 10.2 fusion.26
  494.2 7.0 fusion.54
  501.2 34.3 %collective-permute-done.30 = bf16[256,2048]{1,0:T(8,128)(2,1)} collective-permute-done((bf16[256,2048]{1,0:T(8,128)(2,1)S(1)}, bf16[256,2048]{1,0:T(8,128)(2,1)}, u32[]{:S(2)}, u32[]{:S(2)}) %collective-permute-start.30) | collective-permute-done | bytes 1048608 | tf_op jit(solution)/shard_map/ppermute | solution.py:15
  549.4 10.4 collective-permute-done.27
  572.9 7.2 fusion.53
  598.8 14.3 %multiply_reduce_fusion = (f32[4,512]{1,0:T(4,128)S(1)}, f32[4,512,2048]{2,1,0:T(8,128)}) fusion(f32[4,512,2048]{2,1,0:T(8,128)} %get-tuple-element.177, f32[4,512]{1,0:T(4,128)S(1)} %log_add_fusion, bf16[512,4,128]{0,2,1:T(8,128)(2,1)S(1)} %bitcast.140, bf16[1024,4,128]{0,2,1:T(8,128)(2,1)S(1)} %copy-done.23, bf16[1024,4,128]{0,2,1:T(8,128)(2,1)} %bitcast.5, ...), kind=kOutput, calls=%fused_computation.3 | convolution fusion | flops 1095759872 | bytes 36192256 | tf_op jit(solution)/shard_map/while/body/eval_jaxpr/qhd,khd->hqk/dot_general | solution.py:252
  613.1 15.9 %multiply_convert_fusion = bf16[4,512,2048]{2,1,0:T(8,128)(2,1)} fusion(f32[4,512,2048]{2,1,0:T(8,128)} %get-tuple-element.180, f32[4,512,2048]{2,1,0:T(8,128)} %get-tuple-element.177, f32[4,512]{1,0:T(4,128)S(1)} %get-tuple-element.179, f32[4,512]{1,0:T(4,128)S(1)} %log_add_fusion), kind=kLoop, calls=%fused_computation.2 | loop fusion | flops 16777216 | bytes 41959424 | tf_op jit(solution)/shard_map/while/body/eval_jaxpr/convert_element_type | solution.py:256
  629.0 6.3 fusion.29
  651.3 121.4 %collective-permute-done.46 = bf16[256,2048]{1,0:T(8,128)(2,1)S(1)} collective-permute-done((bf16[256,2048]{1,0:T(8,128)(2,1)S(1)}, bf16[256,2048]{1,0:T(8,128)(2,1)S(1)}, u32[]{:S(2)}, u32[]{:S(2)}) %collective-permute-start.46) | collective-permute-done | bytes 1048608 | tf_op jit(solution)/shard_map/ppermute | solution.py:15
  773.5 21.6 %collective-permute-done.36 = bf16[1024,512]{0,1:T(8,128)(2,1)S(1)} collective-permute-done((bf16[1024,512]{0,1:T(8,128)(2,1)S(1)}, bf16[1024,512]{0,1:T(8,128)(2,1)S(1)}, u32[]{:S(2)}, u32[]{:S(2)}) %collective-permute-start.36) | collective-permute-done | bytes 1048608 | tf_op jit(solution)/shard_map/ppermute | solution.py:15
  795.1 12.9 collective-permute-start.47
  809.4 8.2 collective-permute-done.34
  817.6 12.9 collective-permute-start.37
  831.8 8.3 collective-permute-done.40
  840.1 6.7 collective-permute-start.35
  847.3 7.4 convert_add_fusion.1
  895.4 18.2 %collective-permute-done.42 = bf16[2048,256]{1,0:T(8,128)(2,1)} collective-permute-done((bf16[2048,256]{1,0:T(8,128)(2,1)S(1)}, bf16[2048,256]{1,0:T(8,128)(2,1)}, u32[]{:S(2)}, u32[]{:S(2)}) %collective-permute-start.42) | collective-permute-done | bytes 1048608 | tf_op jit(solution)/shard_map/ppermute | solution.py:15
  916.2 34.8 %collective-permute-done.38 = bf16[256,6144]{1,0:T(8,128)(2,1)} collective-permute-done((bf16[256,6144]{1,0:T(8,128)(2,1)}, bf16[256,6144]{1,0:T(8,128)(2,1)}, u32[]{:S(2)}, u32[]{:S(2)}) %collective-permute-start.38) | collective-permute-done | bytes 3145760 | tf_op jit(solution)/shard_map/ppermute | solution.py:15
  951.0 7.4 convert_add_fusion.2
  974.3 24.9 %collective-permute-done.39 = bf16[128,6144]{1,0:T(8,128)(2,1)} collective-permute-done((bf16[128,6144]{1,0:T(8,128)(2,1)}, bf16[128,6144]{1,0:T(8,128)(2,1)}, u32[]{:S(2)}, u32[]{:S(2)}) %collective-permute-start.39) | collective-permute-done | bytes 1572896 | tf_op jit(solution)/shard_map/ppermute | solution.py:15
  1008.9 17.9 %fusion.113 = (f32[4,17]{1,0:T(4,128)S(1)}, f32[128,4,17]{2,1,0:T(4,128)S(1)}) fusion(bf16[17,128,2048]{2,1,0:T(8,128)(2,1)S(1)} %bitcast.136, f32[128,2048,4]{1,0,2:T(8,128)S(1)} %add_bitcast_fusion), kind=kOutput, calls=%fused_computation.270 | convolution fusion | flops 213918144 | bytes 13142288 | tf_op jit(solution)/shard_map/transpose(jvp(tkj,jtd->ktd))/dot_general | solution.py:35
  1030.2 6.7 add_convert_fusion.1
  1037.0 8.7 convert_add_fusion
  1057.5 17.3 %reduce-scatter.11.cloned.1.call-done = bf16[256,128]{1,0:T(8,128)(2,1)} async-done(((bf16[2048,128]{1,0:T(8,128)(2,1)}), bf16[256,128]{1,0:T(8,128)(2,1)}) %reduce-scatter.11.cloned.1.call-update) | async-done | bytes 65552 | tf_op jit(solution)/shard_map/reduce_scatter | solution.py:328
  1076.2 72.7 %reduce-scatter.9.cloned.1.call-done = bf16[256,128]{1,0:T(8,128)(2,1)} async-done(((bf16[2048,128]{1,0:T(8,128)(2,1)}), bf16[256,128]{1,0:T(8,128)(2,1)}) %reduce-scatter.9.cloned.1.call-update) | async-done | bytes 65552 | tf_op jit(solution)/shard_map/reduce_scatter | solution.py:325
  1155.0 25.5 %fusion = bf16[17,128,2048]{2,0,1:T(8,128)(2,1)} fusion(f32[1,128,2048]{2,0,1:T(1,128)S(1)} %broadcast_in_dim.111, f32[128,4,17]{2,1,0:T(4,128)S(1)} %copy-done.27, f32[128,2048,4]{1,0,2:T(8,128)} %copy-done.18), kind=kOutput, calls=%fused_computation.1 | convolution fusion | flops 222822400 | bytes 14190592 | tf_op jit(solution)/shard_map/transpose(jvp(tkj,jtd->ktd))/dot_general | solution.py:35
  1180.7 13.5 copy.76
  1194.5 52.2 %all-reduce.5 = (f32[2048]{0:T(1024)S(1)}, f32[68,68]{1,0:T(8,128)S(1)}, f32[68]{0:T(128)S(1)}, f32[2048]{0:T(1024)S(1)}, f32[2048]{0:T(1024)S(1)}, /*index=5*/f32[2048]{0:T(1024)S(1)}, f32[2048]{0:T(1024)S(1)}) all-reduce(f32[2048]{0:T(1024)S(1)} %get-tuple-element.133, ...), channel_id=1, replica_groups=mesh['dp'=8,'tensor'=16] {'tensor'}, use_global_device_ids=true, to_apply=%region_17.18 | all-reduce | flops 14932 | bytes 119456 | tf_op jit(solution)/shard_map/psum | solution.py:319
  1246.7 34.9 %all-reduce.6 = (f32[2048]{0:T(1024)}, f32[68,68]{1,0:T(8,128)}, f32[68]{0:T(128)}, f32[2048]{0:T(1024)}, f32[2048]{0:T(1024)}, /*index=5*/f32[2048]{0:T(1024)}, f32[2048]{0:T(1024)}) all-reduce(f32[2048]{0:T(1024)S(1)} %get-tuple-element.147, f32[68,68]{1,0:T(8,128)S(1)} %get-tuple-element.148, ...), channel_id=1, replica_groups=mesh['dp'=8,'tensor'=16] {'dp'}, use_global_device_ids=true, to_apply=%region_18.19 | all-reduce | flops 14932 | bytes 119456 | tf_op jit(solution)/shard_map/psum | solution.py:320
  1283.4 21.2 %reduce-scatter.17.cloned.1.call-done = bf16[512,256]{1,0:T(8,128)(2,1)} async-done(((bf16[512,2048]{1,0:T(8,128)(2,1)}), bf16[512,256]{1,0:T(8,128)(2,1)}) %reduce-scatter.17.cloned.1.call-update) | async-done | bytes 262160 | tf_op jit(solution)/shard_map/reduce_scatter | solution.py:337
  1306.3 82.1 %all-reduce.12.cloned.1.call-done = f32[2048,68]{0,1:T(8,128)} async-done(((f32[2048,68]{0,1:T(8,128)}), f32[2048,68]{0,1:T(8,128)}) %all-reduce.12.cloned.1.call-update) | async-done | bytes 557072 | tf_op jit(solution)/shard_map/psum | solution.py:320
  (436 shorter events, 265.9 us)
Async XLA Ops:
  8.0 1046.4 %reduce-scatter.13.cloned.1.call-start = ((), (), s32[]{:S(2)}) async-start(), calls=%async_computation.11 | async-start | bytes 589824 | tf_op jit(solution)/shard_map/reduce_scatter | solution.py:331
  8.1 68.0 %collective-permute-start.8 = (bf16[2048,128]{1,0:T(8,128)(2,1)}, bf16[2048,128]{1,0:T(8,128)(2,1)}, u32[]{:S(2)}, u32[]{:S(2)}) collective-permute-start(bf16[2048,128]{1,0:T(8,128)(2,1)} %param.28), channel_id=1, source_target_pairs={{0,1},{1,0},{2,3},{3,2},{4,5},{5,4},{6,7},{7,6},{8,9},{9,8},{10,11... | collective-permute-start | bytes 1572872 | tf_op jit(solution)/shard_map/ppermute | solution.py:15
  9.6 37.5 %collective-permute-start.12 = (bf16[2048,128]{1,0:T(8,128)(2,1)}, bf16[2048,128]{1,0:T(8,128)(2,1)}, u32[]{:S(2)}, u32[]{:S(2)}) collective-permute-start(bf16[2048,128]{1,0:T(8,128)(2,1)} %param.29), channel_id=1, source_target_pairs={{0,1},{1,0},{2,3},{3,2},{4,5},{5,4},{6,7},{7,6},{8,9},{9,8},{10,11... | collective-permute-start | bytes 1572872 | tf_op jit(solution)/shard_map/ppermute | solution.py:15
  9.7 61.6 %collective-permute-start.2 = (bf16[2048,128]{1,0:T(8,128)(2,1)}, bf16[2048,128]{1,0:T(8,128)(2,1)}, u32[]{:S(2)}, u32[]{:S(2)}) collective-permute-start(bf16[2048,128]{1,0:T(8,128)(2,1)} %param.30), channel_id=1, source_target_pairs={{0,1},{1,0},{2,3},{3,2},{4,5},{5,4},{6,7},{7,6},{8,9},{9,8},{10,11... | collective-permute-start | bytes 1572872 | tf_op jit(solution)/shard_map/ppermute | solution.py:15
  40.5 37.9 %collective-permute-start = (bf16[128,2048]{1,0:T(8,128)(2,1)S(1)}, bf16[128,2048]{1,0:T(8,128)(2,1)}, u32[]{:S(2)}, u32[]{:S(2)}) collective-permute-start(bf16[128,2048]{1,0:T(8,128)(2,1)S(1)} %multiply_convert_fusion.5), channel_id=1, source_target_pairs={{0,4},{1,5},{2,6},{3,7},{4,0},{5,1},{6,2},{7,3},{8,12},{9,13},{10,... | collective-permute-start | bytes 1572872 | tf_op jit(solution)/shard_map/ppermute | solution.py:15
  49.8 52.7 %collective-permute-start.13 = (bf16[2048,256]{1,0:T(8,128)(2,1)}, bf16[2048,256]{1,0:T(8,128)(2,1)}, u32[]{:S(2)}, u32[]{:S(2)}) collective-permute-start(bf16[2048,256]{1,0:T(8,128)(2,1)} %maximum_select_fusion.29), channel_id=1, source_target_pairs={{0,2},{1,3},{2,0},{3,1},{4,6},{5,7},{6,4},{7,5},{8,10},{9,11},{10,... | collective-permute-start | bytes 3145736 | tf_op jit(solution)/shard_map/ppermute | solution.py:15
  69.9 32.9 %collective-permute-start.11 = (bf16[256,2048]{1,0:T(8,128)(2,1)}, bf16[256,2048]{1,0:T(8,128)(2,1)}, u32[]{:S(2)}, u32[]{:S(2)}) collective-permute-start(bf16[256,2048]{1,0:T(8,128)(2,1)} %maximum_select_fusion.28), channel_id=1, source_target_pairs={{0,8},{1,9},{2,10},{3,11},{4,12},{5,13},{6,14},{7,15},{8,0},{9,1},... | collective-permute-start | bytes 3145736 | tf_op jit(solution)/shard_map/ppermute | solution.py:15
  71.3 29.7 %collective-permute-start.6 = (bf16[128,2048]{1,0:T(8,128)(2,1)S(1)}, bf16[128,2048]{1,0:T(8,128)(2,1)S(1)}, u32[]{:S(2)}, u32[]{:S(2)}) collective-permute-start(bf16[128,2048]{1,0:T(8,128)(2,1)S(1)} %multiply_convert_fusion.4), channel_id=1, source_target_pairs={{0,4},{1,5},{2,6},{3,7},{4,0},{5,1},{6,2},{7,3},{8,12},{9,13},{10,... | collective-permute-start | bytes 1572872 | tf_op jit(solution)/shard_map/ppermute | solution.py:15
  76.1 47.7 %collective-permute-start.3 = (bf16[2048,256]{1,0:T(8,128)(2,1)S(1)}, bf16[2048,256]{1,0:T(8,128)(2,1)S(1)}, u32[]{:S(2)}, u32[]{:S(2)}) collective-permute-start(bf16[2048,256]{1,0:T(8,128)(2,1)S(1)} %maximum_select_fusion.23), channel_id=1, source_target_pairs={{0,2},{1,3},{2,0},{3,1},{4,6},{5,7},{6,4},{7,5},{8,10},{9,11},{10,... | collective-permute-start | bytes 3145736 | tf_op jit(solution)/shard_map/ppermute | solution.py:15
  78.5 67.8 %collective-permute-start.9 = (bf16[2048,256]{1,0:T(8,128)(2,1)S(1)}, bf16[2048,256]{1,0:T(8,128)(2,1)S(1)}, u32[]{:S(2)}, u32[]{:S(2)}) collective-permute-start(bf16[2048,256]{1,0:T(8,128)(2,1)S(1)} %maximum_select_fusion.27), channel_id=1, source_target_pairs={{0,2},{1,3},{2,0},{3,1},{4,6},{5,7},{6,4},{7,5},{8,10},{9,11},{10,... | collective-permute-start | bytes 3145736 | tf_op jit(solution)/shard_map/ppermute | solution.py:15
  101.0 24.2 %collective-permute-start.1 = (bf16[256,2048]{1,0:T(8,128)(2,1)S(1)}, bf16[256,2048]{1,0:T(8,128)(2,1)S(1)}, u32[]{:S(2)}, u32[]{:S(2)}) collective-permute-start(bf16[256,2048]{1,0:T(8,128)(2,1)S(1)} %maximum_select_fusion.22), channel_id=1, source_target_pairs={{0,8},{1,9},{2,10},{3,11},{4,12},{5,13},{6,14},{7,15},{8,0},{9,1},... | collective-permute-start | bytes 3145736 | tf_op jit(solution)/shard_map/ppermute | solution.py:15
  102.5 45.0 %collective-permute-start.7 = (bf16[256,2048]{1,0:T(8,128)(2,1)S(1)}, bf16[256,2048]{1,0:T(8,128)(2,1)S(1)}, u32[]{:S(2)}, u32[]{:S(2)}) collective-permute-start(bf16[256,2048]{1,0:T(8,128)(2,1)S(1)} %maximum_select_fusion.26), channel_id=1, source_target_pairs={{0,8},{1,9},{2,10},{3,11},{4,12},{5,13},{6,14},{7,15},{8,0},{9,1},... | collective-permute-start | bytes 3145736 | tf_op jit(solution)/shard_map/ppermute | solution.py:15
  125.2 102.2 %collective-permute-start.22 = (bf16[2048,512]{1,0:T(8,128)(2,1)}, bf16[2048,512]{1,0:T(8,128)(2,1)}, u32[]{:S(2)}, u32[]{:S(2)}) collective-permute-start(bf16[2048,512]{1,0:T(8,128)(2,1)} %param.32), channel_id=1, source_target_pairs={{0,1},{1,0},{2,3},{3,2},{4,5},{5,4},{6,7},{7,6},{8,9},{9,8},{10,11... | collective-permute-start | bytes 6291464 | tf_op jit(solution)/shard_map/ppermute | solution.py:15
  130.1 38.6 %collective-permute-start.15 = (bf16[1024,512]{0,1:T(8,128)(2,1)S(1)}, bf16[1024,512]{0,1:T(8,128)(2,1)S(1)}, u32[]{:S(2)}, u32[]{:S(2)}) collective-permute-start(bf16[1024,512]{0,1:T(8,128)(2,1)S(1)} %maximum_select_fusion.30), channel_id=1, source_target_pairs={{0,2},{1,3},{2,0},{3,1},{4,6},{5,7},{6,4},{7,5},{8,10},{9,11},{10,... | collective-permute-start | bytes 3145736 | tf_op jit(solution)/shard_map/ppermute | solution.py:15
  146.3 75.9 %collective-permute-start.17 = (bf16[256,2048]{1,0:T(8,128)(2,1)}, bf16[256,2048]{1,0:T(8,128)(2,1)}, u32[]{:S(2)}, u32[]{:S(2)}) collective-permute-start(bf16[256,2048]{1,0:T(8,128)(2,1)} %maximum_select_fusion.32), channel_id=1, source_target_pairs={{0,2},{1,3},{2,0},{3,1},{4,6},{5,7},{6,4},{7,5},{8,10},{9,11},{10,... | collective-permute-start | bytes 3145736 | tf_op jit(solution)/shard_map/ppermute | solution.py:15
  150.2 63.7 %collective-permute-start.5 = (bf16[1024,512]{0,1:T(8,128)(2,1)}, bf16[1024,512]{0,1:T(8,128)(2,1)}, u32[]{:S(2)}, u32[]{:S(2)}) collective-permute-start(bf16[1024,512]{0,1:T(8,128)(2,1)} %maximum_select_fusion.24), channel_id=1, source_target_pairs={{0,2},{1,3},{2,0},{3,1},{4,6},{5,7},{6,4},{7,5},{8,10},{9,11},{10,... | collective-permute-start | bytes 3145736 | tf_op jit(solution)/shard_map/ppermute | solution.py:15
  226.1 23.9 %collective-permute-start.18 = (bf16[256,2048]{1,0:T(8,128)(2,1)S(1)}, bf16[256,2048]{1,0:T(8,128)(2,1)S(1)}, u32[]{:S(2)}, u32[]{:S(2)}) collective-permute-start(bf16[256,2048]{1,0:T(8,128)(2,1)S(1)} %select_convert_fusion.14), channel_id=1, source_target_pairs={{0,8},{1,9},{2,10},{3,11},{4,12},{5,13},{6,14},{7,15},{8,0},{9,1},... | collective-permute-start | bytes 3145736 | tf_op jit(solution)/shard_map/ppermute | solution.py:15
  232.5 131.5 %collective-permute-start.23 = (bf16[2048,1024]{1,0:T(8,128)(2,1)S(1)}, bf16[2048,1024]{1,0:T(8,128)(2,1)S(1)}, u32[]{:S(2)}, u32[]{:S(2)}) collective-permute-start(bf16[2048,1024]{1,0:T(8,128)(2,1)S(1)} %maximum_select_fusion.2), channel_id=1, source_target_pairs={{0,2},{1,3},{2,0},{3,1},{4,6},{5,7},{6,4},{7,5},{8,10},{9,11},{10,... | collective-permute-start | bytes 12582920 | tf_op jit(solution)/shard_map/ppermute | solution.py:15
  250.5 84.6 %collective-permute-start.19 = (bf16[128,2048]{1,0:T(8,128)(2,1)S(1)}, bf16[128,2048]{1,0:T(8,128)(2,1)S(1)}, u32[]{:S(2)}, u32[]{:S(2)}) collective-permute-start(bf16[128,2048]{1,0:T(8,128)(2,1)S(1)} %select_convert_fusion.23), channel_id=1, source_target_pairs={{0,4},{1,5},{2,6},{3,7},{4,0},{5,1},{6,2},{7,3},{8,12},{9,13},{10,... | collective-permute-start | bytes 1572872 | tf_op jit(solution)/shard_map/ppermute | solution.py:15
  252.2 99.7 %collective-permute-start.24 = (bf16[512,2048]{1,0:T(8,128)(2,1)S(1)}, bf16[512,2048]{1,0:T(8,128)(2,1)S(1)}, u32[]{:S(2)}, u32[]{:S(2)}) collective-permute-start(bf16[512,2048]{1,0:T(8,128)(2,1)S(1)} %copy-done.25), channel_id=1, source_target_pairs={{0,1},{1,0},{2,3},{3,2},{4,5},{5,4},{6,7},{7,6},{8,9},{9,8},{10,11... | collective-permute-start | bytes 6291464 | tf_op jit(solution)/shard_map/ppermute | solution.py:15
  355.6 95.3 %collective-permute-start.25 = (bf16[1024,2048]{1,0:T(8,128)(2,1)}, bf16[1024,2048]{1,0:T(8,128)(2,1)}, u32[]{:S(2)}, u32[]{:S(2)}) collective-permute-start(bf16[1024,2048]{1,0:T(8,128)(2,1)} %maximum_select_fusion.3), channel_id=1, source_target_pairs={{0,2},{1,3},{2,0},{3,1},{4,6},{5,7},{6,4},{7,5},{8,10},{9,11},{10,... | collective-permute-start | bytes 12582920 | tf_op jit(solution)/shard_map/ppermute | solution.py:15
  362.2 36.0 %collective-permute-start.29 = (bf16[256,2048]{1,0:T(8,128)(2,1)S(1)}, bf16[256,2048]{1,0:T(8,128)(2,1)}, u32[]{:S(2)}, u32[]{:S(2)}) collective-permute-start(bf16[256,2048]{1,0:T(8,128)(2,1)S(1)} %maximum_select_fusion.34), channel_id=1, source_target_pairs={{0,8},{1,9},{2,10},{3,11},{4,12},{5,13},{6,14},{7,15},{8,0},{9,1},... | collective-permute-start | bytes 3145736 | tf_op jit(solution)/shard_map/ppermute | solution.py:15
  492.5 48.0 %collective-permute-start.26 = (bf16[256,2048]{1,0:T(8,128)(2,1)S(1)}, bf16[256,2048]{1,0:T(8,128)(2,1)}, u32[]{:S(2)}, u32[]{:S(2)}) collective-permute-start(bf16[256,2048]{1,0:T(8,128)(2,1)S(1)} %select_convert_fusion.13), channel_id=1, source_target_pairs={{0,8},{1,9},{2,10},{3,11},{4,12},{5,13},{6,14},{7,15},{8,0},{9,1},... | collective-permute-start | bytes 3145736 | tf_op jit(solution)/shard_map/ppermute | solution.py:15
  493.9 41.7 %collective-permute-start.30 = (bf16[256,2048]{1,0:T(8,128)(2,1)S(1)}, bf16[256,2048]{1,0:T(8,128)(2,1)}, u32[]{:S(2)}, u32[]{:S(2)}) collective-permute-start(bf16[256,2048]{1,0:T(8,128)(2,1)S(1)} %select_convert_fusion.12), channel_id=1, source_target_pairs={{0,8},{1,9},{2,10},{3,11},{4,12},{5,13},{6,14},{7,15},{8,0},{9,1},... | collective-permute-start | bytes 3145736 | tf_op jit(solution)/shard_map/ppermute | solution.py:15
  565.7 281.5 %collective-permute-start.48 = (bf16[2048,1024]{1,0:T(8,128)(2,1)}, bf16[2048,1024]{1,0:T(8,128)(2,1)}, u32[]{:S(2)}, u32[]{:S(2)}) collective-permute-start(bf16[2048,1024]{1,0:T(8,128)(2,1)} %select_convert_fusion.1), channel_id=1, source_target_pairs={{0,2},{1,3},{2,0},{3,1},{4,6},{5,7},{6,4},{7,5},{8,10},{9,11},{10,... | collective-permute-start | bytes 12582920 | tf_op jit(solution)/shard_map/ppermute | solution.py:15
  588.4 448.6 %collective-permute-start.50 = (bf16[1024,2048]{1,0:T(8,128)(2,1)}, bf16[1024,2048]{1,0:T(8,128)(2,1)}, u32[]{:S(2)}, u32[]{:S(2)}) collective-permute-start(bf16[1024,2048]{1,0:T(8,128)(2,1)} %select_convert_fusion), channel_id=1, source_target_pairs={{0,2},{1,3},{2,0},{3,1},{4,6},{5,7},{6,4},{7,5},{8,10},{9,11},{10,... | collective-permute-start | bytes 12582920 | tf_op jit(solution)/shard_map/ppermute | solution.py:15
  642.1 130.6 %collective-permute-start.46 = (bf16[256,2048]{1,0:T(8,128)(2,1)S(1)}, bf16[256,2048]{1,0:T(8,128)(2,1)S(1)}, u32[]{:S(2)}, u32[]{:S(2)}) collective-permute-start(bf16[256,2048]{1,0:T(8,128)(2,1)S(1)} %select_convert_fusion.6), channel_id=1, source_target_pairs={{0,2},{1,3},{2,0},{3,1},{4,6},{5,7},{6,4},{7,5},{8,10},{9,11},{10,... | collective-permute-start | bytes 3145736 | tf_op jit(solution)/shard_map/ppermute | solution.py:15
  643.4 151.7 %collective-permute-start.36 = (bf16[1024,512]{0,1:T(8,128)(2,1)S(1)}, bf16[1024,512]{0,1:T(8,128)(2,1)S(1)}, u32[]{:S(2)}, u32[]{:S(2)}) collective-permute-start(bf16[1024,512]{0,1:T(8,128)(2,1)S(1)} %bitcast.146), channel_id=1, source_target_pairs={{0,2},{1,3},{2,0},{3,1},{4,6},{5,7},{6,4},{7,5},{8,10},{9,11},{10,... | collective-permute-start | bytes 3145736 | tf_op jit(solution)/shard_map/ppermute | solution.py:15
  644.1 173.5 %collective-permute-start.34 = (bf16[1024,512]{0,1:T(8,128)(2,1)S(1)}, bf16[1024,512]{0,1:T(8,128)(2,1)S(1)}, u32[]{:S(2)}, u32[]{:S(2)}) collective-permute-start(bf16[1024,512]{0,1:T(8,128)(2,1)S(1)} %bitcast.145), channel_id=1, source_target_pairs={{0,2},{1,3},{2,0},{3,1},{4,6},{5,7},{6,4},{7,5},{8,10},{9,11},{10,... | collective-permute-start | bytes 3145736 | tf_op jit(solution)/shard_map/ppermute | solution.py:15
  772.7 67.4 %collective-permute-start.40 = (bf16[2048,256]{1,0:T(8,128)(2,1)S(1)}, bf16[2048,256]{1,0:T(8,128)(2,1)S(1)}, u32[]{:S(2)}, u32[]{:S(2)}) collective-permute-start(bf16[2048,256]{1,0:T(8,128)(2,1)S(1)} %select_convert_fusion.9), channel_id=1, source_target_pairs={{0,2},{1,3},{2,0},{3,1},{4,6},{5,7},{6,4},{7,5},{8,10},{9,11},{10,... | collective-permute-start | bytes 3145736 | tf_op jit(solution)/shard_map/ppermute | solution.py:15
  795.1 59.6 %collective-permute-start.47 = (bf16[128,2048]{1,0:T(8,128)(2,1)S(1)}, bf16[128,2048]{1,0:T(8,128)(2,1)}, u32[]{:S(2)}, u32[]{:S(2)}) collective-permute-start(bf16[128,2048]{1,0:T(8,128)(2,1)S(1)} %select_convert_fusion.15), channel_id=1, source_target_pairs={{0,1},{1,0},{2,3},{3,2},{4,5},{5,4},{6,7},{7,6},{8,9},{9,8},{10,11... | collective-permute-start | bytes 1572872 | tf_op jit(solution)/shard_map/ppermute | solution.py:15
  817.6 39.2 %collective-permute-start.37 = (bf16[512,512]{0,1:T(8,128)(2,1)}, bf16[512,512]{0,1:T(8,128)(2,1)}, u32[]{:S(2)}, u32[]{:S(2)}) collective-permute-start(bf16[512,512]{0,1:T(8,128)(2,1)} %select_convert_fusion.19), channel_id=1, source_target_pairs={{0,1},{1,0},{2,3},{3,2},{4,5},{5,4},{6,7},{7,6},{8,9},{9,8},{10,11... | collective-permute-start | bytes 1572872 | tf_op jit(solution)/shard_map/ppermute | solution.py:15
  840.1 28.1 %collective-permute-start.35 = (bf16[512,512]{0,1:T(8,128)(2,1)}, bf16[512,512]{0,1:T(8,128)(2,1)}, u32[]{:S(2)}, u32[]{:S(2)}) collective-permute-start(bf16[512,512]{0,1:T(8,128)(2,1)} %select_convert_fusion.20), channel_id=1, source_target_pairs={{0,1},{1,0},{2,3},{3,2},{4,5},{5,4},{6,7},{7,6},{8,9},{9,8},{10,11... | collective-permute-start | bytes 1572872 | tf_op jit(solution)/shard_map/ppermute | solution.py:15
  847.2 40.4 %collective-permute-start.41 = (bf16[2048,128]{1,0:T(8,128)(2,1)S(1)}, bf16[2048,128]{1,0:T(8,128)(2,1)}, u32[]{:S(2)}, u32[]{:S(2)}) collective-permute-start(bf16[2048,128]{1,0:T(8,128)(2,1)S(1)} %select_convert_fusion.18), channel_id=1, source_target_pairs={{0,1},{1,0},{2,3},{3,2},{4,5},{5,4},{6,7},{7,6},{8,9},{9,8},{10,11... | collective-permute-start | bytes 1572872 | tf_op jit(solution)/shard_map/ppermute | solution.py:15
  856.8 199.2 %reduce-scatter.7.cloned.1.call-start = ((), (), s32[]{:S(2)}) async-start(), calls=%async_computation.8 | async-start | bytes 589824 | tf_op jit(solution)/shard_map/reduce_scatter | solution.py:322
  865.8 25.3 %collective-permute-start.44 = (bf16[2048,256]{1,0:T(8,128)(2,1)}, bf16[2048,256]{1,0:T(8,128)(2,1)}, u32[]{:S(2)}, u32[]{:S(2)}) collective-permute-start(bf16[2048,256]{1,0:T(8,128)(2,1)} %select_convert_fusion.7), channel_id=1, source_target_pairs={{0,2},{1,3},{2,0},{3,1},{4,6},{5,7},{6,4},{7,5},{8,10},{9,11},{10,... | collective-permute-start | bytes 3145736 | tf_op jit(solution)/shard_map/ppermute | solution.py:15
  878.0 73.0 %collective-permute-start.38 = (bf16[256,6144]{1,0:T(8,128)(2,1)}, bf16[256,6144]{1,0:T(8,128)(2,1)}, u32[]{:S(2)}, u32[]{:S(2)}) collective-permute-start(bf16[256,6144]{1,0:T(8,128)(2,1)} %select_convert_fusion.2), channel_id=1, source_target_pairs={{0,8},{1,9},{2,10},{3,11},{4,12},{5,13},{6,14},{7,15},{8,0},{9,1},... | collective-permute-start | bytes 9437192 | tf_op jit(solution)/shard_map/ppermute | solution.py:15
  886.7 26.9 %collective-permute-start.42 = (bf16[2048,256]{1,0:T(8,128)(2,1)S(1)}, bf16[2048,256]{1,0:T(8,128)(2,1)}, u32[]{:S(2)}, u32[]{:S(2)}) collective-permute-start(bf16[2048,256]{1,0:T(8,128)(2,1)S(1)} %select_convert_fusion.8), channel_id=1, source_target_pairs={{0,2},{1,3},{2,0},{3,1},{4,6},{5,7},{6,4},{7,5},{8,10},{9,11},{10,... | collective-permute-start | bytes 3145736 | tf_op jit(solution)/shard_map/ppermute | solution.py:15
  889.8 185.0 %reduce-scatter.11.cloned.1.call-start = ((), (), s32[]{:S(2)}) async-start(), calls=%async_computation.10 | async-start | bytes 589824 | tf_op jit(solution)/shard_map/reduce_scatter | solution.py:328
  894.1 70.4 %collective-permute-start.45 = (bf16[2048,128]{1,0:T(8,128)(2,1)S(1)}, bf16[2048,128]{1,0:T(8,128)(2,1)S(1)}, u32[]{:S(2)}, u32[]{:S(2)}) collective-permute-start(bf16[2048,128]{1,0:T(8,128)(2,1)S(1)} %select_convert_fusion.16), channel_id=1, source_target_pairs={{0,1},{1,0},{2,3},{3,2},{4,5},{5,4},{6,7},{7,6},{8,9},{9,8},{10,11... | collective-permute-start | bytes 1572872 | tf_op jit(solution)/shard_map/ppermute | solution.py:15
  915.3 56.3 %collective-permute-start.43 = (bf16[2048,128]{1,0:T(8,128)(2,1)S(1)}, bf16[2048,128]{1,0:T(8,128)(2,1)}, u32[]{:S(2)}, u32[]{:S(2)}) collective-permute-start(bf16[2048,128]{1,0:T(8,128)(2,1)S(1)} %select_convert_fusion.17), channel_id=1, source_target_pairs={{0,1},{1,0},{2,3},{3,2},{4,5},{5,4},{6,7},{7,6},{8,9},{9,8},{10,11... | collective-permute-start | bytes 1572872 | tf_op jit(solution)/shard_map/ppermute | solution.py:15
  962.5 36.7 %collective-permute-start.39 = (bf16[128,6144]{1,0:T(8,128)(2,1)}, bf16[128,6144]{1,0:T(8,128)(2,1)}, u32[]{:S(2)}, u32[]{:S(2)}) collective-permute-start(bf16[128,6144]{1,0:T(8,128)(2,1)} %select_convert_fusion.5), channel_id=1, source_target_pairs={{0,4},{1,5},{2,6},{3,7},{4,0},{5,1},{6,2},{7,3},{8,12},{9,13},{10,... | collective-permute-start | bytes 4718600 | tf_op jit(solution)/shard_map/ppermute | solution.py:15
  965.5 183.4 %reduce-scatter.9.cloned.1.call-start = ((), (), s32[]{:S(2)}) async-start(), calls=%async_computation.9 | async-start | bytes 589824 | tf_op jit(solution)/shard_map/reduce_scatter | solution.py:325
  970.7 59.5 %collective-permute-start.49 = (bf16[2048,512]{1,0:T(8,128)(2,1)}, bf16[2048,512]{1,0:T(8,128)(2,1)}, u32[]{:S(2)}, u32[]{:S(2)}) collective-permute-start(bf16[2048,512]{1,0:T(8,128)(2,1)} %select_convert_fusion.4), channel_id=1, source_target_pairs={{0,1},{1,0},{2,3},{3,2},{4,5},{5,4},{6,7},{7,6},{8,9},{9,8},{10,11... | collective-permute-start | bytes 6291464 | tf_op jit(solution)/shard_map/ppermute | solution.py:15
  973.8 181.2 %all-reduce.10.cloned.1.call-start = ((), (), s32[]{:S(2)}) async-start(), calls=%async_computation.6 | async-start | bytes 1179648 | tf_op jit(solution)/shard_map/psum | solution.py:319
  1030.2 251.4 %reduce-scatter.15.cloned.1.call-start = ((), (), s32[]{:S(2)}) async-start(), calls=%async_computation.12 | async-start | bytes 2359296 | tf_op jit(solution)/shard_map/reduce_scatter | solution.py:334
  1036.9 267.7 %reduce-scatter.17.cloned.1.call-start = ((), (), s32[]{:S(2)}) async-start(), calls=%async_computation.13 | async-start | bytes 2359296 | tf_op jit(solution)/shard_map/reduce_scatter | solution.py:337
  1054.4 334.0 %all-reduce.12.cloned.1.call-start = ((), (), s32[]{:S(2)}) async-start(), calls=%async_computation.7 | async-start | bytes 1179648 | tf_op jit(solution)/shard_map/psum | solution.py:320
  (113 other events, 1942.0 us)
Sparse Core Ops, SparseCore 0:
  856.9 71.2 reduce-scatter.12
  932.7 69.2 reduce-scatter.6
  1005.5 69.2 reduce-scatter.10
  1079.1 69.7 reduce-scatter.8
  1152.5 74.3 reduce-scatter.14
  1230.5 74.0 reduce-scatter.16
  1307.2 81.1 all-reduce.11
Sparse Core Ops, SparseCore 1:
  1030.2 118.8 all-reduce.9
